TPU v7x, 128 devices: a whole 4x4x4 slice. The times are simulated.
128 devices in a mesh: dp: 16 (over x, y_lo, core), expert: 8 (over y_hi, z).
Axes of the slice: x: 4, y: 4 (y_hi: 2, y_lo: 2; y = y_hi * 2 + y_lo), z: 4, core: 2. Of those that a mesh axis runs over, the one named last changes fastest.
Arguments:
- tokens: bfloat16 [256, 256, 1280], P(('dp', 'expert')), may hold values from -5 to 5, as said below
- slot_param: bfloat16 [32, 1280], replicated, may hold values from -0.1 to 0.1
- inner_weight: bfloat16 [32, 5120, 1280], P('expert', 'dp'), may hold values from -0.15625 to 0.15625
- outer_weight: bfloat16 [32, 5120, 1280], P('expert', 'dp'), may hold values from -0.078125 to 0.078125
- output_grad: bfloat16 [256, 256, 1280], P(('dp', 'expert')), may hold values from -6 to 6
Outputs:
- grad_tokens: bfloat16 [256, 256, 1280], P(('dp', 'expert'))
- grad_param: float32 [32, 1280], replicated
- grad_inner: bfloat16 [32, 5120, 1280], P('expert', 'dp')
- grad_outer: bfloat16 [32, 5120, 1280], P('expert', 'dp')
Inputs may be any that keep to these rules, and one draw needn't show every extreme that they name: `tokens`: saved patch rows of order one.
All inputs are finite; a program needn't handle non-finite values.
Results may differ from a plain program's by a relative error of at most 0.03.
Values may be sent and summed in bfloat16 or wider, within the bound.
A program may use at most 128 MiB of HBM per device.

v0:
```python
import jax
import jax.numpy as jnp
from jax import lax
from jax.sharding import PartitionSpec as P


def gelu_slope(values):
    return (
        0.5 * (1.0 + jax.scipy.special.erf(values * 0.7071067811865476))
        + values * jnp.exp(-0.5 * values * values) * 0.3989422804014327
    )


def on_device(tokens, slot_param, inner_weight, outer_weight, output_grad):
    images = tokens.shape[0]
    model_width = tokens.shape[2]
    groups = lax.axis_size("expert")
    local_experts = inner_weight.shape[0]
    logits = jnp.einsum("sd,bmd->bsm", slot_param, tokens, preferred_element_type=jnp.float32)
    dispatch = jax.nn.softmax(logits, axis=2)
    combine = jax.nn.softmax(logits, axis=1)
    dispatch_low = dispatch.astype(jnp.bfloat16)
    slot_inputs = jnp.einsum(
        "bsm,bmd->bsd", dispatch_low, tokens, preferred_element_type=jnp.float32
    ).astype(jnp.bfloat16)
    slot_grads = jnp.einsum(
        "bsm,bmd->bsd",
        combine.astype(jnp.bfloat16),
        output_grad,
        preferred_element_type=jnp.float32,
    ).astype(jnp.bfloat16)
    shaped = (images, groups, local_experts, model_width)
    slot_inputs = slot_inputs.reshape(shaped)
    slot_grads = slot_grads.reshape(shaped)
    collected = (
        lax.all_gather(slot_inputs, "dp", axis=0, tiled=True),
        lax.all_gather(slot_grads, "dp", axis=0, tiled=True),
    )
    routed = (
        lax.all_to_all(collected[0], "expert", split_axis=1, concat_axis=0, tiled=True),
        lax.all_to_all(collected[1], "expert", split_axis=1, concat_axis=0, tiled=True),
    )
    rows_in, rows_grad = tuple(
        (member.reshape(-1, local_experts, model_width) for member in routed)
    )
    hidden = jnp.einsum("red,efd->efr", rows_in, inner_weight, preferred_element_type=jnp.float32)
    active = jax.nn.gelu(hidden, approximate=False).astype(jnp.bfloat16)
    out_part = jnp.einsum(
        "efr,efd->red", active, outer_weight, preferred_element_type=jnp.float32
    ).astype(jnp.bfloat16)
    active_grad = jnp.einsum(
        "red,efd->efr", rows_grad, outer_weight, preferred_element_type=jnp.float32
    )
    scaled = (active_grad * gelu_slope(hidden)).astype(jnp.bfloat16)
    grad_outer = jnp.einsum(
        "efr,red->efd", active, rows_grad, preferred_element_type=jnp.float32
    ).astype(jnp.bfloat16)
    grad_inner = jnp.einsum(
        "efr,red->efd", scaled, rows_in, preferred_element_type=jnp.float32
    ).astype(jnp.bfloat16)
    back_part = jnp.einsum(
        "efr,efd->red", scaled, inner_weight, preferred_element_type=jnp.float32
    ).astype(jnp.bfloat16)
    lowered = tuple(
        (member.reshape(-1, 1, local_experts, model_width) for member in (out_part, back_part))
    )
    routed_back = (
        lax.all_to_all(lowered[0], "expert", split_axis=0, concat_axis=1, tiled=True),
        lax.all_to_all(lowered[1], "expert", split_axis=0, concat_axis=1, tiled=True),
    )
    summed = (
        lax.psum_scatter(routed_back[0], "dp", scatter_dimension=0, tiled=True).astype(jnp.float32),
        lax.psum_scatter(routed_back[1], "dp", scatter_dimension=0, tiled=True).astype(jnp.float32),
    )
    slot_outputs, slot_backs = tuple((member.astype(jnp.bfloat16) for member in summed))
    slot_outputs = slot_outputs.reshape(images, -1, model_width)
    slot_backs = slot_backs.reshape(images, -1, model_width)
    combine_grad = jnp.einsum(
        "bmd,bsd->bsm", output_grad, slot_outputs, preferred_element_type=jnp.float32
    )
    combine_term = combine * (combine_grad - jnp.sum(combine * combine_grad, axis=1, keepdims=True))
    dispatch_grad = jnp.einsum(
        "bmd,bsd->bsm", tokens, slot_backs, preferred_element_type=jnp.float32
    )
    dispatch_term = dispatch * (
        dispatch_grad - jnp.sum(dispatch * dispatch_grad, axis=2, keepdims=True)
    )
    logit_grad = (combine_term + dispatch_term).astype(jnp.bfloat16)
    grad_tokens = (
        jnp.einsum("bsm,bsd->bmd", dispatch_low, slot_backs, preferred_element_type=jnp.float32)
        + jnp.einsum("bsm,sd->bmd", logit_grad, slot_param, preferred_element_type=jnp.float32)
    ).astype(jnp.bfloat16)
    param_local = jnp.einsum("bsm,bmd->sd", logit_grad, tokens, preferred_element_type=jnp.float32)
    grad_param = lax.psum(param_local, ("dp", "expert"))
    return (grad_tokens, grad_param, grad_inner, grad_outer)


def solution(mesh):
    in_specs = (
        P(("dp", "expert"), None, None),
        P(),
        P("expert", "dp", None),
        P("expert", "dp", None),
        P(("dp", "expert"), None, None),
    )
    out_specs = (
        P(("dp", "expert"), None, None),
        P(),
        P("expert", "dp", None),
        P("expert", "dp", None),
    )
    return jax.shard_map(
        on_device, mesh=mesh, in_specs=in_specs, out_specs=out_specs, check_vma=False
    )
```

profile of v0, /device:TPU:1, one launch (start us, length us, event | category | flops | bytes accessed | tf_op | source)
XLA Modules:
  0.0 487.1 jit_solution(6166446673092790433)
XLA Ops:
  7.2 0.0 all-gather.5.cloned.1.call-start
  7.2 1.9 convolution_bitcast_fusion.3
  9.2 0.7 fusion.52
  9.9 1.7 convolution_convert_fusion.4
  11.6 0.7 reshape.42
  12.3 1.6 copy.26
  13.9 0.0 all-gather.3.cloned.1.call-start
  14.0 0.6 fusion.51
  14.6 1.6 convolution_convert_fusion.5
  16.3 0.7 reshape.40
  17.0 1.6 copy.23
  18.6 33.9 %all-gather.5.cloned.1.call-done = bf16[32,8,4,1280]{3,1,2,0:T(8,128)(2,1)} async-done(((bf16[2,8,4,1280]{3,1,2,0:T(8,128)(2,1)}), bf16[32,8,4,1280]{3,1,2,0:T(8,128)(2,1)}) %all-gather.5.cloned.1.call-update) | async-done | bytes 2621456 | tf_op jit(solution)/shard_map/all_gather | solution.py:36
  52.5 4.2 copy.27
  56.8 6.3 %all-to-all-start.1 = ((bf16[32,8,4,1280]{3,2,0,1:T(4,128)(2,1)}), bf16[32,8,4,1280]{3,2,0,1:T(4,128)(2,1)}, u32[]{:S(2)}, u32[]{:S(2)}) async-start(bf16[32,8,4,1280]{3,2,0,1:T(4,128)(2,1)} %copy.27), calls=%async_computation.1 | async-start | bytes 5242880 | tf_op jit(solution)/shard_map/all_to_all | solution.py:40
  63.0 29.5 %all-gather.3.cloned.1.call-done = bf16[32,8,4,1280]{3,1,2,0:T(8,128)(2,1)} async-done(((bf16[2,8,4,1280]{3,1,2,0:T(8,128)(2,1)}), bf16[32,8,4,1280]{3,1,2,0:T(8,128)(2,1)}) %all-gather.3.cloned.1.call-update) | async-done | bytes 2621456 | tf_op jit(solution)/shard_map/all_gather | solution.py:37
  92.5 4.2 copy.24
  96.8 10.8 %all-to-all-done.1 = bf16[32,8,4,1280]{3,2,0,1:T(4,128)(2,1)} async-done(((bf16[32,8,4,1280]{3,2,0,1:T(4,128)(2,1)}), bf16[32,8,4,1280]{3,2,0,1:T(4,128)(2,1)}, u32[]{:S(2)}, u32[]{:S(2)}) %all-to-all-start.1) | async-done | bytes 2621472 | tf_op jit(solution)/shard_map/all_to_all | solution.py:40
  107.6 4.4 all-to-all-start
  112.0 0.0 reduce-scatter.3.cloned.1.call-start
  112.0 3.7 copy.28
  115.7 28.2 %all-to-all-done = bf16[32,8,4,1280]{3,2,0,1:T(4,128)(2,1)} async-done(((bf16[32,8,4,1280]{3,2,0,1:T(4,128)(2,1)}), bf16[32,8,4,1280]{3,2,0,1:T(4,128)(2,1)}, u32[]{:S(2)}, u32[]{:S(2)}) %all-to-all-start) | async-done | bytes 2621472 | tf_op jit(solution)/shard_map/all_to_all | solution.py:41
  143.9 2.3 copy.25
  146.3 0.2 copy-done.1
  146.5 4.6 fusion.15
  151.1 1.2 fusion.8
  152.3 1.6 fusion.4
  153.9 2.0 copy.29
  155.9 37.3 %all_to_all.66 = bf16[256,1,4,1280]{3,2,1,0:T(4,128)(2,1)S(1)} all-to-all(bf16[256,1,4,1280]{3,2,1,0:T(4,128)(2,1)S(1)} %copy.29), channel_id=1, replica_groups=mesh['dp'=16,'expert'=8] {'expert'}, dimensions={0} | all-to-all | bytes 5242880 | tf_op jit(solution)/shard_map/all_to_all | solution.py:69
  193.2 3.7 copy.47
  197.0 0.0 reduce-scatter.5.cloned.1.call-start
  197.0 3.7 fusion.5
  200.7 2.0 copy.33
  202.7 59.4 %all_to_all.67 = bf16[256,1,4,1280]{3,2,1,0:T(4,128)(2,1)S(1)} all-to-all(bf16[256,1,4,1280]{3,2,1,0:T(4,128)(2,1)S(1)} %copy.33), channel_id=1, replica_groups=mesh['dp'=16,'expert'=8] {'expert'}, dimensions={0} | all-to-all | bytes 5242880 | tf_op jit(solution)/shard_map/all_to_all | solution.py:68
  262.2 3.7 copy.46
  265.8 0.3 all-reduce.2.cloned.1.call-start
  266.1 4.8 convolution_convert_fusion.1
  271.0 2.7 convolution_convert_fusion
  273.7 1.1 copy.31
  274.8 2.4 fusion.36
  277.2 47.6 %reduce-scatter.5.cloned.1.call-done = bf16[2,8,4,1280]{3,1,2,0:T(8,128)(2,1)} async-done(((bf16[32,8,4,1280]{3,1,2,0:T(8,128)(2,1)}), bf16[2,8,4,1280]{3,1,2,0:T(8,128)(2,1)}) %reduce-scatter.5.cloned.1.call-update) | async-done | bytes 163856 | tf_op jit(solution)/shard_map/reduce_scatter | solution.py:72
  324.9 1.1 copy.35
  326.0 2.4 fusion.34
  328.4 0.8 fusion.31
  329.2 3.1 fusion.33
  332.4 2.5 convolution_bitcast_fusion
  334.9 3.4 fusion.6
  338.3 140.7 %all-reduce.2.cloned.1.call-done = f32[32,1280]{1,0:T(8,128)} async-done(((f32[32,1280]{1,0:T(8,128)}), f32[32,1280]{1,0:T(8,128)}) %all-reduce.2.cloned.1.call-update) | async-done | bytes 163856 | tf_op jit(solution)/shard_map/psum | solution.py:94
  479.0 1.6 copy.49
  (23 shorter events, 0.1 us)
Async XLA Ops:
  7.2 139.1 %copy-start = (bf16[4,320,1280]{2,1,0:T(8,128)(2,1)S(1)}, bf16[4,320,1280]{2,1,0:T(8,128)(2,1)}, u32[]{:S(2)}) copy-start(bf16[4,320,1280]{2,1,0:T(8,128)(2,1)} %param.7) | copy-start | bytes 9830404
  7.2 45.3 %all-gather.5.cloned.1.call-start = ((), (), s32[]{:S(2)}) async-start(), calls=%async_computation.7 | async-start | bytes 2785280 | tf_op jit(solution)/shard_map/all_gather | solution.py:36
  13.9 78.6 %all-gather.3.cloned.1.call-start = ((), (), s32[]{:S(2)}) async-start(), calls=%async_computation.6 | async-start | bytes 2785280 | tf_op jit(solution)/shard_map/all_gather | solution.py:37
  56.8 50.8 %all-to-all-start.1 = ((bf16[32,8,4,1280]{3,2,0,1:T(4,128)(2,1)}), bf16[32,8,4,1280]{3,2,0,1:T(4,128)(2,1)}, u32[]{:S(2)}, u32[]{:S(2)}) async-start(bf16[32,8,4,1280]{3,2,0,1:T(4,128)(2,1)} %copy.27), calls=%async_computation.1 | async-start | bytes 5242880 | tf_op jit(solution)/shard_map/all_to_all | solution.py:40
  107.6 36.3 %all-to-all-start = ((bf16[32,8,4,1280]{3,2,0,1:T(4,128)(2,1)}), bf16[32,8,4,1280]{3,2,0,1:T(4,128)(2,1)}, u32[]{:S(2)}, u32[]{:S(2)}) async-start(bf16[32,8,4,1280]{3,2,0,1:T(4,128)(2,1)} %copy.24), calls=%async_computation | async-start | bytes 5242880 | tf_op jit(solution)/shard_map/all_to_all | solution.py:41
  112.0 161.7 %reduce-scatter.3.cloned.1.call-start = ((), (), s32[]{:S(2)}) async-start(), calls=%async_computation.8 | async-start | bytes 2785280 | tf_op jit(solution)/shard_map/reduce_scatter | solution.py:73
  143.9 2.5 copy-start.1
  146.2 4.8 copy-start.2
  146.5 4.6 copy-start.4
  152.3 1.6 copy-start.6
  197.0 127.9 %reduce-scatter.5.cloned.1.call-start = ((), (), s32[]{:S(2)}) async-start(), calls=%async_computation.9 | async-start | bytes 2785280 | tf_op jit(solution)/shard_map/reduce_scatter | solution.py:72
  265.8 213.2 %all-reduce.2.cloned.1.call-start = ((), (), s32[]{:S(2)}) async-start(), calls=%async_computation.10 | async-start | bytes 327680 | tf_op jit(solution)/shard_map/psum | solution.py:94
  266.1 4.8 copy-start.3
  266.1 4.8 copy-start.5
  324.9 3.6 copy-start.7
  324.9 3.6 copy-start.8
Sparse Core Ops, SparseCore 0:
  14.0 38.4 all-gather.4
  54.8 37.6 all-gather.2
  197.1 63.1 reduce-scatter.2
  266.0 58.8 reduce-scatter.4
  335.0 143.9 all-reduce.1
where the time goes:
time: 488 us; the launch traced here: 487 us
  waiting for transfers between devices  291 us (60%)
  blocking collectives  96.8 us (20%)
  matrix products  37.8 us (8%)
  local copies, waits for them, and re-layouts  34.5 us (7%)
  between operations  13.9 us (3%)
  starting transfers between devices  11.1 us (2%)
    psum x1, waiting for transfers between devices, on_device(): grad_param = lax.psum(param_local, ('dp', 'expert'))  141 us
    all_to_all x1, blocking collectives, on_device(): lax.all_to_all(lowered[0], 'expert', split_axis=0, concat_axis=1, tiled=T...  59.4 us
    reduce_scatter x1, waiting for transfers between devices, on_device(): lax.psum_scatter(routed_back[0], 'dp', scatter_dimension=0, tiled=True)  47.6 us
    all_to_all x1, blocking collectives, on_device(): lax.all_to_all(lowered[1], 'expert', split_axis=0, concat_axis=1, tiled=T...  37.3 us
    all_gather x1, waiting for transfers between devices, on_device(): lax.all_gather(slot_inputs, 'dp', axis=0, tiled=True)  33.9 us
    all_gather x1, waiting for transfers between devices, on_device(): lax.all_gather(slot_grads, 'dp', axis=0, tiled=True)  29.5 us
    all_to_all x1, waiting for transfers between devices, on_device(): lax.all_to_all(collected[1], 'expert', split_axis=1, concat_axis=0, tiled...  28.2 us
    all_to_all x1, waiting for transfers between devices, on_device(): lax.all_to_all(collected[0], 'expert', split_axis=1, concat_axis=0, tiled...  10.8 us
  transfers between devices with their start and end apart: 7, of which 6 were waited for; matrix products, arithmetic and copies ran while one was open for 8% of the time, Pallas kernels for 0%

commit v1 on v0

v1 whole, which is shorter than its diff:
```python
import functools

import jax
import jax.numpy as jnp
from jax import lax
from jax.experimental import pallas as pl
from jax.experimental.pallas import tpu as pltpu
from jax.sharding import PartitionSpec as P

MESH = pl.DeviceIdType.MESH
F32 = jnp.float32
BF16 = jnp.bfloat16
NX, NY, NC = 4, 2, 2
GROUPS = 8
LOCAL = 4
IMGS = 2
SLOTS = GROUPS * LOCAL
ROWS = 16
BLOCKS = NC * NY * NX
D = 1280
PATCHES = 256
HIDDEN = 320
TILE = 256
STEPS = D // TILE


def dot(a, b, ca=1, cb=0):
    return lax.dot_general(a, b, (((ca,), (cb,)), ((), ())), preferred_element_type=F32)


def permutation(source_of):
    size = 2 * IMGS * SLOTS
    row = lax.broadcasted_iota(jnp.int32, (size, size), 0)
    column = lax.broadcasted_iota(jnp.int32, (size, size), 1)
    return jnp.where(column == source_of(row), 1.0, 0.0).astype(BF16)


def slots_to_messages(r):
    group, array, expert, image = r // 16, (r // 8) % 2, (r // 2) % 4, r % 2
    return array * 64 + image * 32 + group * 4 + expert


def messages_to_slots(r):
    array, image, group, expert = r // 64, (r // 32) % 2, (r // 4) % 8, r % 4
    return group * 16 + array * 8 + expert * 2 + image


def messages_to_blocks(r):
    array, expert, group, image = r // 64, (r // 16) % 4, (r // 2) % 8, r % 2
    return group * 16 + array * 8 + expert * 2 + image


def blocks_to_messages(r):
    group, array, expert, image = r // 16, (r // 8) % 2, (r // 2) % 4, r % 2
    return array * 64 + expert * 16 + group * 2 + image


def kernel(
    tokens, slot_param, inner, outer, cotangent,
    grad_tokens, grad_param, grad_inner, grad_outer,
    T, G, SP, WI, WO, DI, CO, X, MSG, MSG_IN, BACK, BACK_IN, FIN, SUMS,
    R, PART, SIB, RY0, RX0, RY1, RX1,
    PP, AR1, S1, AR2, S2, AR3, AR4, S4, GP,
    in_sem, a2a_s, a2a_r, back_s, back_r, ag_s, ag_r, rs_s, rs_r, ar_s, ar_r,
):
    dp, ex = lax.axis_index("dp"), lax.axis_index("expert")
    x, y, c = dp // 4, (dp // 2) % 2, dp % 2

    def at_dp(px, py, pc):
        return (px * 4 + py * 2 + pc, ex)

    def right(k):
        return (x + k) % NX

    def left(k):
        return (x + NX - k) % NX

    def to_x(k):
        return at_dp(right(k), y, c)

    to_y = at_dp(x, 1 - y, c)
    to_core = at_dp(x, y, 1 - c)

    def ex_to(k):
        return (ex + k) % GROUPS

    def ex_from(k):
        return (ex + GROUPS - k) % GROUPS

    def remote(src, dst, send, recv, device):
        return pltpu.make_async_remote_copy(
            src_ref=src, dst_ref=dst, send_sem=send, recv_sem=recv, device_id=device, device_id_type=MESH
        )

    barrier = pltpu.get_barrier_semaphore()
    for k in range(1, GROUPS):
        pl.semaphore_signal(barrier, inc=1, device_id=(dp, ex_to(k)), device_id_type=MESH)
    for k in range(1, NX):
        pl.semaphore_signal(barrier, inc=1, device_id=to_x(k), device_id_type=MESH)
    pl.semaphore_signal(barrier, inc=1, device_id=to_y, device_id_type=MESH)
    pl.semaphore_signal(barrier, inc=1, device_id=to_core, device_id_type=MESH)

    loads = [
        pltpu.make_async_copy(slot_param, SP, in_sem.at[0]),
        pltpu.make_async_copy(tokens, T, in_sem.at[1]),
        pltpu.make_async_copy(cotangent, G, in_sem.at[2]),
        pltpu.make_async_copy(inner, WI, in_sem.at[3]),
        pltpu.make_async_copy(outer, WO, in_sem.at[4]),
    ]
    for load in loads:
        load.start()
    for load in loads[:3]:
        load.wait()

    for i in range(IMGS):
        logits = dot(SP[...], T[i], 1, 1)
        ed = jnp.exp(logits - jnp.max(logits, axis=1, keepdims=True))
        dispatch = ed / jnp.sum(ed, axis=1, keepdims=True)
        ec = jnp.exp(logits - jnp.max(logits, axis=0, keepdims=True))
        combine = ec / jnp.sum(ec, axis=0, keepdims=True)
        DI[i] = dispatch
        CO[i] = combine
        X[i] = dot(dispatch.astype(BF16), T[i]).astype(BF16)
        X[IMGS + i] = dot(combine.astype(BF16), G[i]).astype(BF16)
    MSG[...] = (
        dot(permutation(slots_to_messages), X[...].reshape(2 * IMGS * SLOTS, D))
        .astype(BF16).reshape(GROUPS, ROWS, D)
    )

    pl.semaphore_wait(barrier, GROUPS - 1 + NX - 1 + 2)

    def a2a(k):
        return remote(MSG.at[ex_to(k)], MSG_IN.at[ex], a2a_s.at[k], a2a_r.at[k], (dp, ex_to(k)))

    for k in range(1, GROUPS):
        a2a(k).start()
    MSG_IN[ex] = MSG[ex]
    for k in range(1, GROUPS):
        a2a(k).wait_recv()
    blocks = (
        dot(permutation(messages_to_blocks), MSG_IN[...].reshape(2 * IMGS * SLOTS, D))
        .astype(BF16).reshape(2, LOCAL, ROWS, D)
    )
    for a in range(2):
        for e in range(LOCAL):
            R[a, e, c, y, x] = blocks[a, e]

    def block_copy(a, e, py, px, sem, device):
        ref = R.at[a, e, c, py, px]
        return remote(ref, ref, ag_s.at[a, e, sem], ag_r.at[a, e, sem], device)

    def gather_first(e, act):
        for k in range(1, NX):
            act(block_copy(0, e, y, x, k - 1, to_x(k)))
        act(block_copy(1, e, y, x, 3, to_y))
        for k in range(1, NX):
            act(block_copy(1, e, y, x, k - 1, to_x(k)))
        act(block_copy(0, e, y, x, 3, to_y))

    def gather_second_x(e, act, k):
        act(block_copy(1, e, 1 - y, x, 3 + k, to_x(k)))

    def gather_second_y(e, act, k):
        act(block_copy(0, e, y, left(k), 3 + k, to_y))

    def gather_third(e, act):
        for a in range(2):
            ref = R.at[a, e, c]
            act(remote(ref, ref, ag_s.at[a, e, 7], ag_r.at[a, e, 7], to_core))

    def start(copy):
        copy.start()

    def wait_send(copy):
        copy.wait_send()

    def wait_recv(a, e, sem):
        block_copy(a, e, y, x, sem, to_y).wait_recv()

    def second(e):
        wait_recv(1, e, 3)
        for k in range(1, NX):
            gather_second_x(e, start, k)
        for k in (1, 3, 2):
            wait_recv(0, e, k - 1)
            gather_second_y(e, start, k)

    def third(e):
        for sem in (0, 1, 2, 4, 5, 6):
            wait_recv(1, e, sem)
        for sem in (3, 4, 5, 6):
            wait_recv(0, e, sem)
        gather_third(e, start)

    def expert(e):
        for a in range(2):
            ref = R.at[a, e, c]
            remote(ref, ref, ag_s.at[a, e, 7], ag_r.at[a, e, 7], to_core).wait_recv()
        rows_in = R[0, e].reshape(BLOCKS * ROWS, D)
        rows_grad = R[1, e].reshape(BLOCKS * ROWS, D)
        hidden = dot(WI[e], rows_in, 1, 1)
        slope = dot(WO[e], rows_grad, 1, 1)
        phi = 0.5 * (1.0 + lax.erf(hidden * 0.7071067811865476))
        active = (hidden * phi).astype(BF16)
        scaled = (slope * (phi + hidden * jnp.exp(-0.5 * hidden * hidden) * 0.3989422804014327)).astype(BF16)
        active_t = active.T
        scaled_t = scaled.T
        for n in range(STEPS):
            cols = slice(n * TILE, (n + 1) * TILE)
            PART[0, e, :, :, :, :, cols] = (
                dot(active_t, WO[e, :, cols]).astype(BF16).reshape(NC, NY, NX, ROWS, TILE)
            )
            PART[1, e, :, :, :, :, cols] = (
                dot(scaled_t, WI[e, :, cols]).astype(BF16).reshape(NC, NY, NX, ROWS, TILE)
            )
        sums_core(e, start)
        for n in range(STEPS):
            cols = slice(n * TILE, (n + 1) * TILE)
            grad_outer[e, :, cols] = dot(active, rows_grad[:, cols]).astype(BF16)
            grad_inner[e, :, cols] = dot(scaled, rows_in[:, cols]).astype(BF16)

    def sum_copy(a, e, src, dst, sem, device):
        return remote(src, dst, rs_s.at[a, e, sem], rs_r.at[a, e, sem], device)

    def sums_core(e, act):
        for a in range(2):
            act(sum_copy(a, e, PART.at[a, e, 1 - c], SIB.at[a, e], 0, to_core))

    def sums_y0(e):
        return sum_copy(0, e, PART.at[0, e, c, 1 - y], RY0.at[e], 4, to_y)

    def sums_x0(e, k):
        return sum_copy(0, e, PART.at[0, e, c, y, right(k)], RX0.at[e, k - 1], k, to_x(k))

    def sums_x1(e, k):
        return sum_copy(1, e, PART.at[1, e, c, :, right(k)], RX1.at[e, k - 1], k, to_x(k))

    def sums_y1(e):
        return sum_copy(1, e, PART.at[1, e, c, 1 - y, x], RY1.at[e], 4, to_y)

    def add_core(e):
        for a in range(2):
            sum_copy(a, e, PART.at[a, e, 1 - c], SIB.at[a, e], 0, to_core).wait_recv()
        for a in range(2):
            PART[a, e, c] = (PART[a, e, c].astype(F32) + SIB[a, e].astype(F32)).astype(BF16)
            if a == 0:
                sums_y0(e).start()
            else:
                for k in range(1, NX):
                    sums_x1(e, k).start()

    def add_second(e):
        sums_y0(e).wait_recv()
        PART[0, e, c, y] = (PART[0, e, c, y].astype(F32) + RY0[e].astype(F32)).astype(BF16)
        for k in range(1, NX):
            sums_x0(e, k).start()
        total = PART[1, e, c, :, x].astype(F32)
        for k in range(1, NX):
            sums_x1(e, k).wait_recv()
            total = total + RX1[e, k - 1].astype(F32)
        PART[1, e, c, :, x] = total.astype(BF16)
        sums_y1(e).start()

    def add_third(e):
        total = PART[0, e, c, y, x].astype(F32)
        for k in range(1, NX):
            sums_x0(e, k).wait_recv()
            total = total + RX0[e, k - 1].astype(F32)
        FIN[0, e] = total.astype(BF16)
        sums_y1(e).wait_recv()
        FIN[1, e] = (PART[1, e, c, y, x].astype(F32) + RY1[e].astype(F32)).astype(BF16)

    def firsts(e, carry):
        gather_first(e, start)
        return carry

    lax.fori_loop(0, LOCAL, firsts, 0)
    for load in loads[3:]:
        load.wait()

    def step(t, carry):
        def stage(lag, work):
            @pl.when(jnp.logical_and(t >= lag, t < LOCAL + lag))
            def _():
                work(t - lag)

        stage(0, second)
        stage(1, third)
        stage(3, add_core)
        stage(4, add_second)
        stage(5, add_third)
        stage(2, expert)
        return carry

    lax.fori_loop(0, LOCAL + 5, step, 0)

    BACK[...] = (
        dot(permutation(blocks_to_messages), FIN[...].reshape(2 * IMGS * SLOTS, D))
        .astype(BF16).reshape(GROUPS, ROWS, D)
    )

    def back(k):
        return remote(BACK.at[ex_to(k)], BACK_IN.at[ex], back_s.at[k], back_r.at[k], (dp, ex_to(k)))

    for k in range(1, GROUPS):
        back(k).start()
    BACK_IN[ex] = BACK[ex]
    for k in range(1, GROUPS):
        back(k).wait_recv()
    SUMS[...] = (
        dot(permutation(messages_to_slots), BACK_IN[...].reshape(2 * IMGS * SLOTS, D))
        .astype(BF16).reshape(2, IMGS, SLOTS, D)
    )

    param = jnp.zeros((SLOTS, D), F32)
    logit_grads = []
    for i in range(IMGS):
        dispatch, combine = DI[i], CO[i]
        combine_grad = dot(SUMS[0, i], G[i], 1, 1)
        dispatch_grad = dot(SUMS[1, i], T[i], 1, 1)
        combine_term = combine * (combine_grad - jnp.sum(combine * combine_grad, axis=0, keepdims=True))
        dispatch_term = dispatch * (dispatch_grad - jnp.sum(dispatch * dispatch_grad, axis=1, keepdims=True))
        logit_grad = (combine_term + dispatch_term).astype(BF16)
        logit_grads.append(logit_grad)
        param = param + dot(logit_grad, T[i])

    for j in range(GROUPS):
        PP[j] = param[8 * (j // 2):8 * (j // 2) + 8, 640 * (j % 2):640 * (j % 2) + 640]

    def ar_scatter(k):
        return remote(PP.at[ex_to(k)], AR1.at[k - 1], ar_s.at[k], ar_r.at[k], (dp, ex_to(k)))

    for k in range(1, GROUPS):
        ar_scatter(k).start()

    for i in range(IMGS):
        both = jnp.concatenate([DI[i].astype(BF16), logit_grads[i]], axis=0)
        rows = jnp.concatenate([SUMS[1, i], SP[...]], axis=0)
        grad_tokens[i] = dot(both.T, rows).astype(BF16)

    total = PP[ex]
    for k in range(1, GROUPS):
        ar_scatter(k).wait_recv()
        total = total + AR1[k - 1]
    S1[...] = total
    ar_core = remote(S1, AR2, ar_s.at[8], ar_r.at[8], to_core)
    ar_core.start()
    ar_core.wait_recv()
    S2[...] = S1[...] + AR2[...]
    ar_y = remote(S2, AR3, ar_s.at[9], ar_r.at[9], to_y)
    ar_y.start()
    ar_y.wait_recv()
    AR4[x] = S2[...] + AR3[...]

    def ar_x(k):
        return remote(AR4.at[x], AR4.at[x], ar_s.at[9 + k], ar_r.at[9 + k], to_x(k))

    for k in range(1, NX):
        ar_x(k).start()
    for k in range(1, NX):
        ar_x(k).wait_recv()
    GP[ex] = (AR4[0] + AR4[1]) + (AR4[2] + AR4[3])

    def ar_gather(k):
        return remote(GP.at[ex], GP.at[ex], ar_s.at[12 + k], ar_r.at[12 + k], (dp, ex_to(k)))

    for k in range(1, GROUPS):
        ar_gather(k).start()

    def drain(e, carry):
        gather_first(e, wait_send)
        for k in range(1, NX):
            gather_second_x(e, wait_send, k)
            gather_second_y(e, wait_send, k)
            sums_x0(e, k).wait_send()
            sums_x1(e, k).wait_send()
        gather_third(e, wait_send)
        sums_core(e, wait_send)
        sums_y0(e).wait_send()
        sums_y1(e).wait_send()
        return carry

    lax.fori_loop(0, LOCAL, drain, 0)
    for k in range(1, GROUPS):
        a2a(k).wait_send()
        back(k).wait_send()
        ar_scatter(k).wait_send()
    ar_core.wait_send()
    ar_y.wait_send()
    for k in range(1, NX):
        ar_x(k).wait_send()
    for k in range(1, GROUPS):
        ar_gather(k).wait_recv()
    for k in range(1, GROUPS):
        ar_gather(k).wait_send()
    for j in range(GROUPS):
        grad_param[8 * (j // 2):8 * (j // 2) + 8, 640 * (j % 2):640 * (j % 2) + 640] = GP[j]


def on_device(tokens, slot_param, inner_weight, outer_weight, output_grad):
    vmem = pl.BlockSpec(memory_space=pltpu.VMEM)
    chunk = (8, D * SLOTS // (8 * GROUPS))
    dma = pltpu.SemaphoreType.DMA
    return pl.pallas_call(
        kernel,
        out_shape=(
            jax.ShapeDtypeStruct(tokens.shape, BF16),
            jax.ShapeDtypeStruct(slot_param.shape, F32),
            jax.ShapeDtypeStruct(inner_weight.shape, BF16),
            jax.ShapeDtypeStruct(outer_weight.shape, BF16),
        ),
        in_specs=[pl.BlockSpec(memory_space=pl.ANY)] * 5,
        out_specs=(vmem,) * 4,
        scratch_shapes=[
            pltpu.VMEM((IMGS, PATCHES, D), BF16),
            pltpu.VMEM((IMGS, PATCHES, D), BF16),
            pltpu.VMEM((SLOTS, D), BF16),
            pltpu.VMEM((LOCAL, HIDDEN, D), BF16),
            pltpu.VMEM((LOCAL, HIDDEN, D), BF16),
            pltpu.VMEM((IMGS, SLOTS, PATCHES), F32),
            pltpu.VMEM((IMGS, SLOTS, PATCHES), F32),
            pltpu.VMEM((2 * IMGS, SLOTS, D), BF16),
            pltpu.VMEM((GROUPS, ROWS, D), BF16),
            pltpu.VMEM((GROUPS, ROWS, D), BF16),
            pltpu.VMEM((GROUPS, ROWS, D), BF16),
            pltpu.VMEM((GROUPS, ROWS, D), BF16),
            pltpu.VMEM((2, LOCAL, ROWS, D), BF16),
            pltpu.VMEM((2, IMGS, SLOTS, D), BF16),
            pltpu.VMEM((2, LOCAL, NC, NY, NX, ROWS, D), BF16),
            pltpu.VMEM((2, LOCAL, NC, NY, NX, ROWS, D), BF16),
            pltpu.VMEM((2, LOCAL, NY, NX, ROWS, D), BF16),
            pltpu.VMEM((LOCAL, NX, ROWS, D), BF16),
            pltpu.VMEM((LOCAL, NX - 1, ROWS, D), BF16),
            pltpu.VMEM((LOCAL, ROWS, D), BF16),
            pltpu.VMEM((LOCAL, NX - 1, NY, ROWS, D), BF16),
            pltpu.VMEM((GROUPS,) + chunk, F32),
            pltpu.VMEM((GROUPS - 1,) + chunk, F32),
            pltpu.VMEM(chunk, F32),
            pltpu.VMEM(chunk, F32),
            pltpu.VMEM(chunk, F32),
            pltpu.VMEM(chunk, F32),
            pltpu.VMEM((NX,) + chunk, F32),
            pltpu.VMEM(chunk, F32),
            pltpu.VMEM((GROUPS,) + chunk, F32),
            dma((5,)), dma((GROUPS,)), dma((GROUPS,)), dma((GROUPS,)), dma((GROUPS,)),
            dma((2, LOCAL, 8)), dma((2, LOCAL, 8)), dma((2, LOCAL, 5)), dma((2, LOCAL, 5)),
            dma((20,)), dma((20,)),
        ],
        compiler_params=pltpu.CompilerParams(
            collective_id=0, has_side_effects=True, vmem_limit_bytes=56 * 2**20
        ),
    )(tokens, slot_param, inner_weight, outer_weight, output_grad)


def solution(mesh):
    in_specs = (
        P(("dp", "expert"), None, None),
        P(),
        P("expert", "dp", None),
        P("expert", "dp", None),
        P(("dp", "expert"), None, None),
    )
    out_specs = (
        P(("dp", "expert"), None, None),
        P(),
        P("expert", "dp", None),
        P("expert", "dp", None),
    )
    return jax.shard_map(
        on_device, mesh=mesh, in_specs=in_specs, out_specs=out_specs, check_vma=False
    )
```

time: 488 us -> 106 us (0.22)
  waiting for transfers between devices: 291 us -> 0 us
  blocking collectives: 96.8 us -> 0 us
  Pallas kernels: 0 us -> 94.6 us
  matrix products: 37.8 us -> 0 us
  local copies, waits for them, and re-layouts: 34.5 us -> 9.75 us
  between operations: 13.9 us -> 0.64 us
  starting transfers between devices: 11.1 us -> 0 us
    psum x1 -> x0, waiting for transfers between devices: 141 us -> none  [on_device(): grad_param = lax.psum(param_local, ('dp', 'expert'))]
    all_to_all x2 -> x0, blocking collectives: 96.8 us -> none  [the longest x1 59.4 us: on_device(): lax.all_to_all(lowered[0], 'expert', split_axis=0, concat_axis=1, tiled=T...]
    pallas_call x0 -> x1, Pallas kernels: none -> 94.6 us  [on_device(): pl.pallas_call(kernel, out_shape=(jax.ShapeDtypeStruct(tokens.shape, BF16...]
    all_gather x2 -> x0, waiting for transfers between devices: 63.4 us -> none  [the longest x1 33.9 us: on_device(): lax.all_gather(slot_inputs, 'dp', axis=0, tiled=True)]
    reduce_scatter x2 -> x0, waiting for transfers between devices: 47.7 us -> none  [the longest x1 47.6 us: on_device(): lax.psum_scatter(routed_back[0], 'dp', scatter_dimension=0, tiled=True)]
    all_to_all x2 -> x0, waiting for transfers between devices: 39 us -> none  [the longest x1 28.2 us: on_device(): lax.all_to_all(collected[1], 'expert', split_axis=1, concat_axis=0, tiled...]
    dot_general x14 -> x0, matrix products: 37.8 us -> none  [the longest x1 4.82 us: on_device(): jnp.einsum('efr,red->efd', scaled, rows_in, preferred_element_type=jnp.fl...]
    all_to_all x4 -> x0, local copies, waits for them, and re-layouts: 13.3 us -> none  [the longest x1 3.68 us: on_device(): lax.all_to_all(collected[0], 'expert', split_axis=1, concat_axis=0, tiled...]
  transfers between devices with their start and end apart: 7 -> 0, of which waited for: 6 -> 0; matrix products, arithmetic and copies ran while one was open for 8% -> 0% of each run, Pallas kernels for 0% -> 0%
where the time goes in v1:
time: 106 us; the launch traced here: 105 us
  Pallas kernels  94.6 us (89%)
  local copies, waits for them, and re-layouts  9.75 us (9%)
    pallas_call x1, Pallas kernels, on_device(): pl.pallas_call(kernel, out_shape=(jax.ShapeDtypeStruct(tokens.shape, BF16...  94.6 us
    unnamed x6, local copies, waits for them, and re-layouts  9.75 us

profile of v1, /device:TPU:1, one launch (start us, length us, event | category | flops | bytes accessed | tf_op | source)
XLA Modules:
  0.0 105.0 jit_solution(2925371415378056637)
XLA Ops:
  0.6 94.6 %shard_map.84 = (bf16[2,256,1280]{2,1,0:T(8,128)(2,1)}, f32[32,1280]{1,0:T(8,128)}, bf16[4,320,1280]{2,1,0:T(8,128)(2,1)}, bf16[4,320,1280]{2,1,0:T(8,128)(2,1)}) custom-call(bf16[2,256,1280]{2,1,0:T(8,128)(2,1)} %tokens.1, bf16[32,1280]{1,0:T(8,128)(2,1)} %slot_param.1, bf16[4,320,1280]{2,1,0:T(8,128)(2,1)} %inner.1, bf16[4,320,1280]{2,1,0:T(8,128)(2,1)} %outer.1, ...), custom_call_target="tpu_custom_call" | custom-call | tf_op jit(solution)/shard_map/pallas_call | solution.py:404
  95.3 2.5 %copy.13 = bf16[2,256,1280]{2,1,0:T(8,128)(2,1)} copy(bf16[2,256,1280]{2,1,0:T(8,128)(2,1)} %get-tuple-element.8) | data formatting | bytes 2621440
  97.7 1.6 %copy.14 = f32[32,1280]{1,0:T(8,128)} copy(f32[32,1280]{1,0:T(8,128)} %get-tuple-element.9) | data formatting | bytes 327680
  99.3 0.0 copy-start
  99.3 4.0 %copy.15 = bf16[4,320,1280]{2,1,0:T(8,128)(2,1)} copy(bf16[4,320,1280]{2,1,0:T(8,128)(2,1)} %get-tuple-element.10) | data formatting | bytes 6553600
  103.3 0.0 copy-done
  103.3 1.7 %copy.16 = bf16[4,320,1280]{2,1,0:T(8,128)(2,1)} copy(bf16[4,320,1280]{2,1,0:T(8,128)(2,1)S(1)} %copy-done) | data formatting | bytes 6553600
Async XLA Ops:
  99.3 4.0 %copy-start = (bf16[4,320,1280]{2,1,0:T(8,128)(2,1)S(1)}, bf16[4,320,1280]{2,1,0:T(8,128)(2,1)}, u32[]{:S(2)}) copy-start(bf16[4,320,1280]{2,1,0:T(8,128)(2,1)} %get-tuple-element.11) | copy-start | bytes 9830404

commit v2 on v1

--- a/solution.py
+++ b/solution.py
@@ -59,7 +59,7 @@
     tokens, slot_param, inner, outer, cotangent,
     grad_tokens, grad_param, grad_inner, grad_outer,
     T, G, SP, WI, WO, DI, CO, X, MSG, MSG_IN, BACK, BACK_IN, FIN, SUMS,
-    R, PART, SIB, RY0, RX0, RY1, RX1,
+    R, ACT, SCA, PART, SIB, RY0, RX0, RY1, RX1,
     PP, AR1, S1, AR2, S2, AR3, AR4, S4, GP,
     in_sem, a2a_s, a2a_r, back_s, back_r, ag_s, ag_r, rs_s, rs_r, ar_s, ar_r,
 ):
@@ -213,11 +213,17 @@
             PART[1, e, :, :, :, :, cols] = (
                 dot(scaled_t, WI[e, :, cols]).astype(BF16).reshape(NC, NY, NX, ROWS, TILE)
             )
+        ACT[e] = active
+        SCA[e] = scaled
         sums_core(e, start)
+
+    def weight_grads(e):
         for n in range(STEPS):
             cols = slice(n * TILE, (n + 1) * TILE)
-            grad_outer[e, :, cols] = dot(active, rows_grad[:, cols]).astype(BF16)
-            grad_inner[e, :, cols] = dot(scaled, rows_in[:, cols]).astype(BF16)
+            rows_in = R[0, e, :, :, :, :, cols].reshape(BLOCKS * ROWS, TILE)
+            rows_grad = R[1, e, :, :, :, :, cols].reshape(BLOCKS * ROWS, TILE)
+            grad_outer[e, :, cols] = dot(ACT[e], rows_grad).astype(BF16)
+            grad_inner[e, :, cols] = dot(SCA[e], rows_in).astype(BF16)
 
     def sum_copy(a, e, src, dst, sem, device):
         return remote(src, dst, rs_s.at[a, e, sem], rs_r.at[a, e, sem], device)
@@ -270,11 +276,8 @@
         sums_y1(e).wait_recv()
         FIN[1, e] = (PART[1, e, c, y, x].astype(F32) + RY1[e].astype(F32)).astype(BF16)
 
-    def firsts(e, carry):
-        gather_first(e, start)
-        return carry
-
-    lax.fori_loop(0, LOCAL, firsts, 0)
+    gather_first(0, start)
+    gather_first(1, start)
     for load in loads[3:]:
         load.wait()
 
@@ -285,11 +288,13 @@
                 work(t - lag)
 
         stage(0, second)
+        stage(-2, lambda e: gather_first(e, start))
         stage(1, third)
         stage(3, add_core)
         stage(4, add_second)
         stage(5, add_third)
         stage(2, expert)
+        stage(6, weight_grads)
         return carry
 
     lax.fori_loop(0, LOCAL + 5, step, 0)
@@ -305,6 +310,7 @@
     for k in range(1, GROUPS):
         back(k).start()
     BACK_IN[ex] = BACK[ex]
+    weight_grads(LOCAL - 1)
     for k in range(1, GROUPS):
         back(k).wait_recv()
     SUMS[...] = (
@@ -397,19 +403,27 @@
         grad_param[8 * (j // 2):8 * (j // 2) + 8, 640 * (j % 2):640 * (j % 2) + 640] = GP[j]
 
 
+def write_out(*refs):
+    copies = [pltpu.make_async_copy(refs[i], refs[4 + i], refs[8].at[i]) for i in range(4)]
+    for copy in copies:
+        copy.start()
+    for copy in copies:
+        copy.wait()
+
+
 def on_device(tokens, slot_param, inner_weight, outer_weight, output_grad):
     vmem = pl.BlockSpec(memory_space=pltpu.VMEM)
     chunk = (8, D * SLOTS // (8 * GROUPS))
     dma = pltpu.SemaphoreType.DMA
-    return pl.pallas_call(
+    results = pl.pallas_call(
         kernel,
         out_shape=(
-            jax.ShapeDtypeStruct(tokens.shape, BF16),
-            jax.ShapeDtypeStruct(slot_param.shape, F32),
-            jax.ShapeDtypeStruct(inner_weight.shape, BF16),
-            jax.ShapeDtypeStruct(outer_weight.shape, BF16),
+            pltpu.VMEM(tokens.shape, BF16),
+            pltpu.VMEM(slot_param.shape, F32),
+            pltpu.VMEM(inner_weight.shape, BF16),
+            pltpu.VMEM(outer_weight.shape, BF16),
         ),
-        in_specs=[pl.BlockSpec(memory_space=pl.ANY)] * 5,
+        in_specs=[pl.BlockSpec(memory_space=pltpu.HBM)] * 5,
         out_specs=(vmem,) * 4,
         scratch_shapes=[
             pltpu.VMEM((IMGS, PATCHES, D), BF16),
@@ -427,6 +441,8 @@
             pltpu.VMEM((2, LOCAL, ROWS, D), BF16),
             pltpu.VMEM((2, IMGS, SLOTS, D), BF16),
             pltpu.VMEM((2, LOCAL, NC, NY, NX, ROWS, D), BF16),
+            pltpu.VMEM((LOCAL, HIDDEN, BLOCKS * ROWS), BF16),
+            pltpu.VMEM((LOCAL, HIDDEN, BLOCKS * ROWS), BF16),
             pltpu.VMEM((2, LOCAL, NC, NY, NX, ROWS, D), BF16),
             pltpu.VMEM((2, LOCAL, NY, NX, ROWS, D), BF16),
             pltpu.VMEM((LOCAL, NX, ROWS, D), BF16),
@@ -447,9 +463,17 @@
             dma((20,)), dma((20,)),
         ],
         compiler_params=pltpu.CompilerParams(
-            collective_id=0, has_side_effects=True, vmem_limit_bytes=56 * 2**20
+            collective_id=0, has_side_effects=True, vmem_limit_bytes=54 * 2**20
         ),
     )(tokens, slot_param, inner_weight, outer_weight, output_grad)
+    return pl.pallas_call(
+        write_out,
+        out_shape=tuple(jax.ShapeDtypeStruct(result.shape, result.dtype) for result in results),
+        in_specs=[vmem] * 4,
+        out_specs=(pl.BlockSpec(memory_space=pltpu.HBM),) * 4,
+        scratch_shapes=[dma((4,))],
+        compiler_params=pltpu.CompilerParams(vmem_limit_bytes=2**20),
+    )(*[pltpu.with_memory_space_constraint(result, pltpu.VMEM) for result in results])
 
 
 def solution(mesh):

time: 106 us -> 92.9 us (0.88)
  local copies, waits for them, and re-layouts: 9.75 us -> 0 us
  Pallas kernels: 94.6 us -> 91.9 us
    unnamed x6 -> x0, local copies, waits for them, and re-layouts: 9.75 us -> none
    pallas_call x1 -> x2, Pallas kernels: 94.6 us -> 91.9 us  [the longest x1 88.6 us: on_device(): pl.pallas_call(kernel, out_shape=(pltpu.VMEM(tokens.shape, BF16), pltpu.V...]
where the time goes in v2:
time: 92.9 us; the launch traced here: 92.5 us
  Pallas kernels  91.9 us (99%)
    pallas_call x1, Pallas kernels, on_device(): pl.pallas_call(kernel, out_shape=(pltpu.VMEM(tokens.shape, BF16), pltpu.V...  88.6 us
    pallas_call x1, Pallas kernels, on_device(): pl.pallas_call(write_out, out_shape=tuple((jax.ShapeDtypeStruct(result.sh...  3.31 us

profile of v2, /device:TPU:1, one launch (start us, length us, event | category | flops | bytes accessed | tf_op | source)
XLA Modules:
  0.0 92.5 jit_solution(16363228795266425167)
XLA Ops:
  0.6 88.6 %shard_map.84 = (bf16[2,256,1280]{2,1,0:T(8,128)(2,1)S(1)}, f32[32,1280]{1,0:T(8,128)S(1)}, bf16[4,320,1280]{2,1,0:T(8,128)(2,1)S(1)}, bf16[4,320,1280]{2,1,0:T(8,128)(2,1)S(1)}) custom-call(bf16[2,256,1280]{2,1,0:T(8,128)(2,1)} %tokens.1, bf16[32,1280]{1,0:T(8,128)(2,1)} %slot_param.1, bf16[4,320,1280]{2,1,0:T(8,128)(2,1)} %inner.1, ...), custom_call_target="tpu_custom_call" | custom-call | tf_op jit(solution)/shard_map/pallas_call | solution.py:418
  89.2 3.3 %shard_map.85 = (bf16[2,256,1280]{2,1,0:T(8,128)(2,1)}, f32[32,1280]{1,0:T(8,128)}, bf16[4,320,1280]{2,1,0:T(8,128)(2,1)}, bf16[4,320,1280]{2,1,0:T(8,128)(2,1)}) custom-call(bf16[2,256,1280]{2,1,0:T(8,128)(2,1)S(1)} %get-tuple-element.8.refs_0_, f32[32,1280]{1,0:T(8,128)S(1)} %get-tuple-element.9.refs_1_, ...), custom_call_target="tpu_custom_call" | custom-call | tf_op jit(solution)/shard_map/pallas_call | solution.py:469

commit v3 on v2

--- a/solution.py
+++ b/solution.py
@@ -11,7 +11,8 @@
 F32 = jnp.float32
 BF16 = jnp.bfloat16
 NX, NY, NC = 4, 2, 2
-GROUPS = 8
+NH, NZ = 2, 4
+GROUPS = NH * NZ
 LOCAL = 4
 IMGS = 2
 SLOTS = GROUPS * LOCAL
@@ -23,6 +24,25 @@
 TILE = 256
 STEPS = D // TILE
 
+ORDER = (
+    "G00 G10 G02 G11",
+    "G13 G01 S00 G12",
+    "S02 S10 G03 T00",
+    "S11 S12 S01 X00",
+    "O10 S13 T02 C00",
+    "O11 O12 T10 S03",
+    "X02 T01 X10 T12",
+    "C02 O13 T11 X01",
+    "C10 X12 D00 X11",
+    "C01 C12 T03 C11",
+    "T13 D10 X03 X13",
+    "D02 C13 C03 D12",
+    "E10 D11 E00 D13",
+    "D01 D03 E02 F10",
+    "E11 E12 E13 E01",
+    "F12 F13 F11 E03",
+)
+
 
 def dot(a, b, ca=1, cb=0):
     return lax.dot_general(a, b, (((ca,), (cb,)), ((), ())), preferred_element_type=F32)
@@ -59,12 +79,13 @@
     tokens, slot_param, inner, outer, cotangent,
     grad_tokens, grad_param, grad_inner, grad_outer,
     T, G, SP, WI, WO, DI, CO, X, MSG, MSG_IN, BACK, BACK_IN, FIN, SUMS,
-    R, ACT, SCA, PART, SIB, RY0, RX0, RY1, RX1,
-    PP, AR1, S1, AR2, S2, AR3, AR4, S4, GP,
-    in_sem, a2a_s, a2a_r, back_s, back_r, ag_s, ag_r, rs_s, rs_r, ar_s, ar_r,
+    R, ACT, SCA, SLOPE, PART, SIB, RY0, RX0, RY1, RX1,
+    PP, AR1, AR2, GP,
+    in_sem, a2a_s, a2a_r, back_s, back_r, ag_s, ag_r, rs_s, rs_r, ar_s, ar_r, mid_s, mid_r, last_s, last_r,
 ):
     dp, ex = lax.axis_index("dp"), lax.axis_index("expert")
     x, y, c = dp // 4, (dp // 2) % 2, dp % 2
+    h, z = ex // NZ, ex % NZ
 
     def at_dp(px, py, pc):
         return (px * 4 + py * 2 + pc, ex)
@@ -92,13 +113,26 @@
             src_ref=src, dst_ref=dst, send_sem=send, recv_sem=recv, device_id=device, device_id_type=MESH
         )
 
+    member = c * NZ + z
+    plane = (x * NY + y) * NH + h
+
+    def to_member(k):
+        other = (member + k) % GROUPS
+        return other, ((x * NY + y) * NC + other // NZ, h * NZ + other % NZ)
+
+    def to_plane(k):
+        other = (plane + k) % (NX * NY * NH)
+        return (other // NH * NC + c, other % NH * NZ + z)
+
     barrier = pltpu.get_barrier_semaphore()
-    for k in range(1, GROUPS):
-        pl.semaphore_signal(barrier, inc=1, device_id=(dp, ex_to(k)), device_id_type=MESH)
-    for k in range(1, NX):
-        pl.semaphore_signal(barrier, inc=1, device_id=to_x(k), device_id_type=MESH)
-    pl.semaphore_signal(barrier, inc=1, device_id=to_y, device_id_type=MESH)
-    pl.semaphore_signal(barrier, inc=1, device_id=to_core, device_id_type=MESH)
+    partners = [(dp, ex_to(k)) for k in range(1, GROUPS)] + [to_core]
+    partners += [(at_dp(x, y, 1 - c)[0], h * NZ + (z + k) % NZ) for k in range(1, NZ)]
+    partners += [
+        (at_dp(right(dx), (y + dy) % NY, c)[0], (h + dh) % NH * NZ + z)
+        for dx in range(NX) for dy in range(NY) for dh in range(NH) if dx or dy
+    ]
+    for partner in partners:
+        pl.semaphore_signal(barrier, inc=1, device_id=partner, device_id_type=MESH)
 
     loads = [
         pltpu.make_async_copy(slot_param, SP, in_sem.at[0]),
@@ -127,7 +161,7 @@
         .astype(BF16).reshape(GROUPS, ROWS, D)
     )
 
-    pl.semaphore_wait(barrier, GROUPS - 1 + NX - 1 + 2)
+    pl.semaphore_wait(barrier, len(partners))
 
     def a2a(k):
         return remote(MSG.at[ex_to(k)], MSG_IN.at[ex], a2a_s.at[k], a2a_r.at[k], (dp, ex_to(k)))
@@ -149,13 +183,13 @@
         ref = R.at[a, e, c, py, px]
         return remote(ref, ref, ag_s.at[a, e, sem], ag_r.at[a, e, sem], device)
 
-    def gather_first(e, act):
-        for k in range(1, NX):
-            act(block_copy(0, e, y, x, k - 1, to_x(k)))
-        act(block_copy(1, e, y, x, 3, to_y))
-        for k in range(1, NX):
-            act(block_copy(1, e, y, x, k - 1, to_x(k)))
-        act(block_copy(0, e, y, x, 3, to_y))
+    def gather_first(a, e, act):
+        if a == 1:
+            act(block_copy(1, e, y, x, 3, to_y))
+        for k in range(1, NX) if a == 0 else (1, 3):
+            act(block_copy(a, e, y, x, k - 1, to_x(k)))
+        if a == 0:
+            act(block_copy(0, e, y, x, 3, to_y))
 
     def gather_second_x(e, act, k):
         act(block_copy(1, e, 1 - y, x, 3 + k, to_x(k)))
@@ -163,10 +197,15 @@
     def gather_second_y(e, act, k):
         act(block_copy(0, e, y, left(k), 3 + k, to_y))
 
-    def gather_third(e, act):
-        for a in range(2):
-            ref = R.at[a, e, c]
-            act(remote(ref, ref, ag_s.at[a, e, 7], ag_r.at[a, e, 7], to_core))
+    def gather_on_right(e, act):
+        act(block_copy(1, e, y, left(1), 1, to_x(1)))
+
+    def gather_on_left(e, act):
+        act(block_copy(1, e, 1 - y, right(1), 5, to_x(3)))
+
+    def gather_third(a, e):
+        ref = R.at[a, e, c]
+        return remote(ref, ref, ag_s.at[a, e, 7], ag_r.at[a, e, 7], to_core)
 
     def start(copy):
         copy.start()
@@ -177,45 +216,45 @@
     def wait_recv(a, e, sem):
         block_copy(a, e, y, x, sem, to_y).wait_recv()
 
-    def second(e):
-        wait_recv(1, e, 3)
-        for k in range(1, NX):
-            gather_second_x(e, start, k)
-        for k in (1, 3, 2):
-            wait_recv(0, e, k - 1)
-            gather_second_y(e, start, k)
-
-    def third(e):
-        for sem in (0, 1, 2, 4, 5, 6):
-            wait_recv(1, e, sem)
-        for sem in (3, 4, 5, 6):
-            wait_recv(0, e, sem)
-        gather_third(e, start)
-
-    def expert(e):
-        for a in range(2):
-            ref = R.at[a, e, c]
-            remote(ref, ref, ag_s.at[a, e, 7], ag_r.at[a, e, 7], to_core).wait_recv()
-        rows_in = R[0, e].reshape(BLOCKS * ROWS, D)
-        rows_grad = R[1, e].reshape(BLOCKS * ROWS, D)
-        hidden = dot(WI[e], rows_in, 1, 1)
-        slope = dot(WO[e], rows_grad, 1, 1)
-        phi = 0.5 * (1.0 + lax.erf(hidden * 0.7071067811865476))
-        active = (hidden * phi).astype(BF16)
-        scaled = (slope * (phi + hidden * jnp.exp(-0.5 * hidden * hidden) * 0.3989422804014327)).astype(BF16)
-        active_t = active.T
-        scaled_t = scaled.T
+    def second(a, e):
+        if a == 0:
+            for k in (1, 3, 2):
+                wait_recv(0, e, k - 1)
+                gather_second_y(e, start, k)
+        else:
+            wait_recv(1, e, 3)
+            for k in (1, 3):
+                gather_second_x(e, start, k)
+            wait_recv(1, e, 0)
+            gather_on_right(e, start)
+
+    def second_on(a, e):
+        wait_recv(1, e, 6)
+        gather_on_left(e, start)
+
+    def third(a, e):
+        for sem in (3, 4, 5, 6) if a == 0 else (2, 1, 4, 5):
+            wait_recv(a, e, sem)
+        gather_third(a, e).start()
+
+    def expert(a, e):
+        gather_third(a, e).wait_recv()
+        rows = R[a, e].reshape(BLOCKS * ROWS, D)
+        if a == 0:
+            hidden = dot(WI[e], rows, 1, 1)
+            phi = 0.5 * (1.0 + lax.erf(hidden * 0.7071067811865476))
+            SLOPE[e] = phi + hidden * jnp.exp(-0.5 * hidden * hidden) * 0.3989422804014327
+            act, kept, weight = (hidden * phi).astype(BF16), ACT, WO
+        else:
+            act, kept, weight = (dot(WO[e], rows, 1, 1) * SLOPE[e]).astype(BF16), SCA, WI
+        kept[e] = act
+        act_t = act.T
         for n in range(STEPS):
             cols = slice(n * TILE, (n + 1) * TILE)
-            PART[0, e, :, :, :, :, cols] = (
-                dot(active_t, WO[e, :, cols]).astype(BF16).reshape(NC, NY, NX, ROWS, TILE)
+            PART[a, e, :, :, :, :, cols] = (
+                dot(act_t, weight[e, :, cols]).astype(BF16).reshape(NC, NY, NX, ROWS, TILE)
             )
-            PART[1, e, :, :, :, :, cols] = (
-                dot(scaled_t, WI[e, :, cols]).astype(BF16).reshape(NC, NY, NX, ROWS, TILE)
-            )
-        ACT[e] = active
-        SCA[e] = scaled
-        sums_core(e, start)
+        sums_core(a, e).start()
 
     def weight_grads(e):
         for n in range(STEPS):
@@ -228,9 +267,8 @@
     def sum_copy(a, e, src, dst, sem, device):
         return remote(src, dst, rs_s.at[a, e, sem], rs_r.at[a, e, sem], device)
 
-    def sums_core(e, act):
-        for a in range(2):
-            act(sum_copy(a, e, PART.at[a, e, 1 - c], SIB.at[a, e], 0, to_core))
+    def sums_core(a, e):
+        return sum_copy(a, e, PART.at[a, e, 1 - c], SIB.at[a, e], 0, to_core)
 
     def sums_y0(e):
         return sum_copy(0, e, PART.at[0, e, c, 1 - y], RY0.at[e], 4, to_y)
@@ -241,63 +279,69 @@
     def sums_x1(e, k):
         return sum_copy(1, e, PART.at[1, e, c, :, right(k)], RX1.at[e, k - 1], k, to_x(k))
 
+    def sums_on_right(e):
+        return sum_copy(1, e, PART.at[1, e, c, y, right(2)], RX1.at[e, 1, 0], 2, to_x(1))
+
+    def sums_on_left(e):
+        return sum_copy(1, e, PART.at[1, e, c, 1 - y, right(2)], RX1.at[e, 1, 1], 5, to_x(3))
+
     def sums_y1(e):
         return sum_copy(1, e, PART.at[1, e, c, 1 - y, x], RY1.at[e], 4, to_y)
 
-    def add_core(e):
-        for a in range(2):
-            sum_copy(a, e, PART.at[a, e, 1 - c], SIB.at[a, e], 0, to_core).wait_recv()
-        for a in range(2):
-            PART[a, e, c] = (PART[a, e, c].astype(F32) + SIB[a, e].astype(F32)).astype(BF16)
-            if a == 0:
-                sums_y0(e).start()
-            else:
-                for k in range(1, NX):
-                    sums_x1(e, k).start()
-
-    def add_second(e):
-        sums_y0(e).wait_recv()
-        PART[0, e, c, y] = (PART[0, e, c, y].astype(F32) + RY0[e].astype(F32)).astype(BF16)
-        for k in range(1, NX):
-            sums_x0(e, k).start()
-        total = PART[1, e, c, :, x].astype(F32)
-        for k in range(1, NX):
-            sums_x1(e, k).wait_recv()
-            total = total + RX1[e, k - 1].astype(F32)
-        PART[1, e, c, :, x] = total.astype(BF16)
-        sums_y1(e).start()
-
-    def add_third(e):
-        total = PART[0, e, c, y, x].astype(F32)
-        for k in range(1, NX):
-            sums_x0(e, k).wait_recv()
-            total = total + RX0[e, k - 1].astype(F32)
-        FIN[0, e] = total.astype(BF16)
+    def add(a, b):
+        return (a.astype(F32) + b.astype(F32)).astype(BF16)
+
+    def add_core(a, e):
+        sums_core(a, e).wait_recv()
+        PART[a, e, c] = add(PART[a, e, c], SIB[a, e])
+        if a == 0:
+            sums_y0(e).start()
+        else:
+            sums_on_right(e).start()
+            sums_on_left(e).start()
+
+    def add_second(a, e):
+        if a == 0:
+            sums_y0(e).wait_recv()
+            PART[0, e, c, y] = add(PART[0, e, c, y], RY0[e])
+            for k in range(1, NX):
+                sums_x0(e, k).start()
+        else:
+            sums_on_right(e).wait_recv()
+            PART[1, e, c, y, right(1)] = add(PART[1, e, c, y, right(1)], RX1[e, 1, 0])
+            sums_on_left(e).wait_recv()
+            PART[1, e, c, 1 - y, left(1)] = add(PART[1, e, c, 1 - y, left(1)], RX1[e, 1, 1])
+            for k in (1, 3):
+                sums_x1(e, k).start()
+
+    def add_third(a, e):
+        if a == 0:
+            total = PART[0, e, c, y, x].astype(F32)
+            for k in range(1, NX):
+                sums_x0(e, k).wait_recv()
+                total = total + RX0[e, k - 1].astype(F32)
+            FIN[0, e] = total.astype(BF16)
+        else:
+            total = PART[1, e, c, :, x].astype(F32)
+            for k in (1, 3):
+                sums_x1(e, k).wait_recv()
+                total = total + RX1[e, k - 1].astype(F32)
+            PART[1, e, c, :, x] = total.astype(BF16)
+            sums_y1(e).start()
+
+    def add_fourth(a, e):
         sums_y1(e).wait_recv()
-        FIN[1, e] = (PART[1, e, c, y, x].astype(F32) + RY1[e].astype(F32)).astype(BF16)
-
-    gather_first(0, start)
-    gather_first(1, start)
+        FIN[1, e] = add(PART[1, e, c, y, x], RY1[e])
+
     for load in loads[3:]:
         load.wait()
-
-    def step(t, carry):
-        def stage(lag, work):
-            @pl.when(jnp.logical_and(t >= lag, t < LOCAL + lag))
-            def _():
-                work(t - lag)
-
-        stage(0, second)
-        stage(-2, lambda e: gather_first(e, start))
-        stage(1, third)
-        stage(3, add_core)
-        stage(4, add_second)
-        stage(5, add_third)
-        stage(2, expert)
-        stage(6, weight_grads)
-        return carry
-
-    lax.fori_loop(0, LOCAL + 5, step, 0)
+    steps = {
+        "G": lambda a, e: gather_first(a, e, start), "S": second, "O": second_on, "T": third, "X": expert,
+        "C": add_core, "D": add_second, "E": add_third, "F": add_fourth,
+    }
+    for line in ORDER:
+        for word in line.split():
+            steps[word[0]](int(word[1]), int(word[2]))
 
     BACK[...] = (
         dot(permutation(blocks_to_messages), FIN[...].reshape(2 * IMGS * SLOTS, D))
@@ -310,7 +354,12 @@
     for k in range(1, GROUPS):
         back(k).start()
     BACK_IN[ex] = BACK[ex]
-    weight_grads(LOCAL - 1)
+
+    def grads(e, carry):
+        weight_grads(e)
+        return carry
+
+    lax.fori_loop(0, LOCAL, grads, 0)
     for k in range(1, GROUPS):
         back(k).wait_recv()
     SUMS[...] = (
@@ -334,7 +383,14 @@
         PP[j] = param[8 * (j // 2):8 * (j // 2) + 8, 640 * (j % 2):640 * (j % 2) + 640]
 
     def ar_scatter(k):
-        return remote(PP.at[ex_to(k)], AR1.at[k - 1], ar_s.at[k], ar_r.at[k], (dp, ex_to(k)))
+        other, device = to_member(k)
+        return remote(PP.at[other], AR1.at[k - 1], ar_s.at[k], ar_r.at[k], device)
+
+    def ar_plane(k):
+        return remote(AR2.at[plane], AR2.at[plane], mid_s.at[k], mid_r.at[k], to_plane(k))
+
+    def ar_gather(k):
+        return remote(GP.at[member], GP.at[member], last_s.at[k], last_r.at[k], to_member(k)[1])
 
     for k in range(1, GROUPS):
         ar_scatter(k).start()
@@ -344,44 +400,37 @@
         rows = jnp.concatenate([SUMS[1, i], SP[...]], axis=0)
         grad_tokens[i] = dot(both.T, rows).astype(BF16)
 
-    total = PP[ex]
+    total = PP[member]
     for k in range(1, GROUPS):
         ar_scatter(k).wait_recv()
         total = total + AR1[k - 1]
-    S1[...] = total
-    ar_core = remote(S1, AR2, ar_s.at[8], ar_r.at[8], to_core)
-    ar_core.start()
-    ar_core.wait_recv()
-    S2[...] = S1[...] + AR2[...]
-    ar_y = remote(S2, AR3, ar_s.at[9], ar_r.at[9], to_y)
-    ar_y.start()
-    ar_y.wait_recv()
-    AR4[x] = S2[...] + AR3[...]
-
-    def ar_x(k):
-        return remote(AR4.at[x], AR4.at[x], ar_s.at[9 + k], ar_r.at[9 + k], to_x(k))
-
-    for k in range(1, NX):
-        ar_x(k).start()
-    for k in range(1, NX):
-        ar_x(k).wait_recv()
-    GP[ex] = (AR4[0] + AR4[1]) + (AR4[2] + AR4[3])
-
-    def ar_gather(k):
-        return remote(GP.at[ex], GP.at[ex], ar_s.at[12 + k], ar_r.at[12 + k], (dp, ex_to(k)))
-
+    AR2[plane] = total
+    for k in range(1, NX * NY * NH):
+        ar_plane(k).start()
+    for k in range(1, NX * NY * NH):
+        ar_plane(k).wait_recv()
+    total = AR2[0]
+    for k in range(1, NX * NY * NH):
+        total = total + AR2[k]
+    GP[member] = total
     for k in range(1, GROUPS):
         ar_gather(k).start()
 
     def drain(e, carry):
-        gather_first(e, wait_send)
+        for a in range(2):
+            gather_first(a, e, wait_send)
+            gather_third(a, e).wait_send()
+            sums_core(a, e).wait_send()
+        gather_on_right(e, wait_send)
+        gather_on_left(e, wait_send)
         for k in range(1, NX):
-            gather_second_x(e, wait_send, k)
             gather_second_y(e, wait_send, k)
             sums_x0(e, k).wait_send()
+        for k in (1, 3):
+            gather_second_x(e, wait_send, k)
             sums_x1(e, k).wait_send()
-        gather_third(e, wait_send)
-        sums_core(e, wait_send)
+        sums_on_right(e).wait_send()
+        sums_on_left(e).wait_send()
         sums_y0(e).wait_send()
         sums_y1(e).wait_send()
         return carry
@@ -391,10 +440,8 @@
         a2a(k).wait_send()
         back(k).wait_send()
         ar_scatter(k).wait_send()
-    ar_core.wait_send()
-    ar_y.wait_send()
-    for k in range(1, NX):
-        ar_x(k).wait_send()
+    for k in range(1, NX * NY * NH):
+        ar_plane(k).wait_send()
     for k in range(1, GROUPS):
         ar_gather(k).wait_recv()
     for k in range(1, GROUPS):
@@ -443,6 +490,7 @@
             pltpu.VMEM((2, LOCAL, NC, NY, NX, ROWS, D), BF16),
             pltpu.VMEM((LOCAL, HIDDEN, BLOCKS * ROWS), BF16),
             pltpu.VMEM((LOCAL, HIDDEN, BLOCKS * ROWS), BF16),
+            pltpu.VMEM((LOCAL, HIDDEN, BLOCKS * ROWS), F32),
             pltpu.VMEM((2, LOCAL, NC, NY, NX, ROWS, D), BF16),
             pltpu.VMEM((2, LOCAL, NY, NX, ROWS, D), BF16),
             pltpu.VMEM((LOCAL, NX, ROWS, D), BF16),
@@ -451,16 +499,12 @@
             pltpu.VMEM((LOCAL, NX - 1, NY, ROWS, D), BF16),
             pltpu.VMEM((GROUPS,) + chunk, F32),
             pltpu.VMEM((GROUPS - 1,) + chunk, F32),
-            pltpu.VMEM(chunk, F32),
-            pltpu.VMEM(chunk, F32),
-            pltpu.VMEM(chunk, F32),
-            pltpu.VMEM(chunk, F32),
-            pltpu.VMEM((NX,) + chunk, F32),
-            pltpu.VMEM(chunk, F32),
+            pltpu.VMEM((NX * NY * NH,) + chunk, F32),
             pltpu.VMEM((GROUPS,) + chunk, F32),
             dma((5,)), dma((GROUPS,)), dma((GROUPS,)), dma((GROUPS,)), dma((GROUPS,)),
-            dma((2, LOCAL, 8)), dma((2, LOCAL, 8)), dma((2, LOCAL, 5)), dma((2, LOCAL, 5)),
-            dma((20,)), dma((20,)),
+            dma((2, LOCAL, 8)), dma((2, LOCAL, 8)), dma((2, LOCAL, 6)), dma((2, LOCAL, 6)),
+            dma((GROUPS,)), dma((GROUPS,)), dma((NX * NY * NH,)), dma((NX * NY * NH,)),
+            dma((GROUPS,)), dma((GROUPS,)),
         ],
         compiler_params=pltpu.CompilerParams(
             collective_id=0, has_side_effects=True, vmem_limit_bytes=54 * 2**20

time: 92.9 us -> 87.8 us (0.945)
  Pallas kernels: 91.9 us -> 87 us
    pallas_call x1, Pallas kernels: 88.6 us -> 83.7 us  [on_device(): pl.pallas_call(kernel, out_shape=(pltpu.VMEM(tokens.shape, BF16), pltpu.V...]
where the time goes in v3:
time: 87.8 us; the launch traced here: 87.7 us
  Pallas kernels  87 us (99%)
    pallas_call x1, Pallas kernels, on_device(): pl.pallas_call(kernel, out_shape=(pltpu.VMEM(tokens.shape, BF16), pltpu.V...  83.7 us
    pallas_call x1, Pallas kernels, on_device(): pl.pallas_call(write_out, out_shape=tuple((jax.ShapeDtypeStruct(result.sh...  3.31 us

profile of v3, /device:TPU:1, one launch (start us, length us, event | category | flops | bytes accessed | tf_op | source)
XLA Modules:
  0.0 87.7 jit_solution(10309191200048204260)
XLA Ops:
  0.6 83.7 %shard_map.84 = (bf16[2,256,1280]{2,1,0:T(8,128)(2,1)S(1)}, f32[32,1280]{1,0:T(8,128)S(1)}, bf16[4,320,1280]{2,1,0:T(8,128)(2,1)S(1)}, bf16[4,320,1280]{2,1,0:T(8,128)(2,1)S(1)}) custom-call(bf16[2,256,1280]{2,1,0:T(8,128)(2,1)} %tokens.1, bf16[32,1280]{1,0:T(8,128)(2,1)} %slot_param.1, bf16[4,320,1280]{2,1,0:T(8,128)(2,1)} %inner.1, ...), custom_call_target="tpu_custom_call" | custom-call | tf_op jit(solution)/shard_map/pallas_call | solution.py:465
  84.3 3.3 %shard_map.85 = (bf16[2,256,1280]{2,1,0:T(8,128)(2,1)}, f32[32,1280]{1,0:T(8,128)}, bf16[4,320,1280]{2,1,0:T(8,128)(2,1)}, bf16[4,320,1280]{2,1,0:T(8,128)(2,1)}) custom-call(bf16[2,256,1280]{2,1,0:T(8,128)(2,1)S(1)} %get-tuple-element.8.refs_0_, f32[32,1280]{1,0:T(8,128)S(1)} %get-tuple-element.9.refs_1_, ...), custom_call_target="tpu_custom_call" | custom-call | tf_op jit(solution)/shard_map/pallas_call | solution.py:513

commit v4 on v3

--- a/solution.py
+++ b/solution.py
@@ -23,24 +23,28 @@
 HIDDEN = 320
 TILE = 256
 STEPS = D // TILE
+PARTS = 2
+SLOT_ROWS = 2 * IMGS * SLOTS
+SHARE = SLOTS * D // (8 * 128 * GROUPS)
 
 ORDER = (
-    "G00 G10 G02 G11",
-    "G13 G01 S00 G12",
-    "S02 S10 G03 T00",
-    "S11 S12 S01 X00",
-    "O10 S13 T02 C00",
-    "O11 O12 T10 S03",
-    "X02 T01 X10 T12",
-    "C02 O13 T11 X01",
-    "C10 X12 D00 X11",
-    "C01 C12 T03 C11",
-    "T13 D10 X03 X13",
-    "D02 C13 C03 D12",
-    "E10 D11 E00 D13",
-    "D01 D03 E02 F10",
+    "A00 G00 G11 G10",
+    "G01 A01 G02 G12",
+    "S00 S11 G13 S01",
+    "S10 G03 T00 S12",
+    "S02 O11 X00 O10",
+    "T01 C00 S13 O12",
+    "T11 X01 S03 T02",
+    "T10 X11 O13 C01",
+    "X02 T12 C11 X10",
+    "D00 X12 C10 T03",
+    "T13 C12 C02 D11",
+    "X03 X13 D01 C03",
+    "C13 D12 D10 E00",
+    "D13 D02 D03 E10",
     "E11 E12 E13 E01",
-    "F12 F13 F11 E03",
+    "F10 F11 B00 E02",
+    "F12 E03 F13 B01",
 )
 
 
@@ -48,31 +52,26 @@
     return lax.dot_general(a, b, (((ca,), (cb,)), ((), ())), preferred_element_type=F32)
 
 
-def permutation(source_of):
-    size = 2 * IMGS * SLOTS
-    row = lax.broadcasted_iota(jnp.int32, (size, size), 0)
-    column = lax.broadcasted_iota(jnp.int32, (size, size), 1)
-    return jnp.where(column == source_of(row), 1.0, 0.0).astype(BF16)
-
-
-def slots_to_messages(r):
-    group, array, expert, image = r // 16, (r // 8) % 2, (r // 2) % 4, r % 2
-    return array * 64 + image * 32 + group * 4 + expert
-
-
-def messages_to_slots(r):
-    array, image, group, expert = r // 64, (r // 32) % 2, (r // 4) % 8, r % 4
-    return group * 16 + array * 8 + expert * 2 + image
-
-
-def messages_to_blocks(r):
-    array, expert, group, image = r // 64, (r // 16) % 4, (r // 2) % 8, r % 2
-    return group * 16 + array * 8 + expert * 2 + image
-
-
-def blocks_to_messages(r):
-    group, array, expert, image = r // 16, (r // 8) % 2, (r // 2) % 4, r % 2
-    return array * 64 + expert * 16 + group * 2 + image
+def place(rows, columns, source_of, part, half, transposed=False):
+    shape = (columns, rows) if transposed else (rows, columns)
+    row = lax.broadcasted_iota(jnp.int32, shape, 1 if transposed else 0)
+    column = lax.broadcasted_iota(jnp.int32, shape, 0 if transposed else 1)
+    source, in_half = source_of(row, part, half)
+    return jnp.where(jnp.logical_and(column == source, in_half), 1.0, 0.0).astype(BF16)
+
+
+def slots_of_message(r, part, half):
+    group, array, expert, image = r // 16, (r // 4) % 2, (r // 2) % 2, r % 2
+    return array * 64 + image * 32 + group * 4 + 2 * part + expert, (r // 8) % 2 == half
+
+
+def message_of_blocks(r, part, half):
+    array, expert, group, image = r // 32, (r // 16) % 2, (r // 2) % 8, r % 2
+    return group * 16 + half * 8 + array * 4 + expert * 2 + image, r >= 0
+
+
+def halves(array):
+    return array[:, : D // 2], array[:, D // 2 :]
 
 
 def kernel(
@@ -125,12 +124,12 @@
         return (other // NH * NC + c, other % NH * NZ + z)
 
     barrier = pltpu.get_barrier_semaphore()
-    partners = [(dp, ex_to(k)) for k in range(1, GROUPS)] + [to_core]
-    partners += [(at_dp(x, y, 1 - c)[0], h * NZ + (z + k) % NZ) for k in range(1, NZ)]
-    partners += [
+    partners = [
         (at_dp(right(dx), (y + dy) % NY, c)[0], (h + dh) % NH * NZ + z)
-        for dx in range(NX) for dy in range(NY) for dh in range(NH) if dx or dy
+        for dx in (2, 1, 3, 0) for dh in (1, 0) for dy in (1, 0) if dx or dy
     ]
+    partners += [(dp, ex_to(k)) for k in range(GROUPS - 1, 0, -1)]
+    partners += [(at_dp(x, y, 1 - c)[0], h * NZ + (z + k) % NZ) for k in range(1, NZ)] + [to_core]
     for partner in partners:
         pl.semaphore_signal(barrier, inc=1, device_id=partner, device_id_type=MESH)
 
@@ -156,28 +155,34 @@
         CO[i] = combine
         X[i] = dot(dispatch.astype(BF16), T[i]).astype(BF16)
         X[IMGS + i] = dot(combine.astype(BF16), G[i]).astype(BF16)
-    MSG[...] = (
-        dot(permutation(slots_to_messages), X[...].reshape(2 * IMGS * SLOTS, D))
-        .astype(BF16).reshape(GROUPS, ROWS, D)
-    )
+    flat = halves(X[...].reshape(SLOT_ROWS, D))
+    for part in range(PARTS):
+        rows = [dot(place(SLOT_ROWS, SLOT_ROWS, slots_of_message, part, j), flat[j]) for j in range(2)]
+        MSG[part] = (rows[0] + rows[1]).astype(BF16).reshape(GROUPS, ROWS, D // 2)
 
     pl.semaphore_wait(barrier, len(partners))
 
-    def a2a(k):
-        return remote(MSG.at[ex_to(k)], MSG_IN.at[ex], a2a_s.at[k], a2a_r.at[k], (dp, ex_to(k)))
-
-    for k in range(1, GROUPS):
-        a2a(k).start()
-    MSG_IN[ex] = MSG[ex]
-    for k in range(1, GROUPS):
-        a2a(k).wait_recv()
-    blocks = (
-        dot(permutation(messages_to_blocks), MSG_IN[...].reshape(2 * IMGS * SLOTS, D))
-        .astype(BF16).reshape(2, LOCAL, ROWS, D)
-    )
-    for a in range(2):
-        for e in range(LOCAL):
-            R[a, e, c, y, x] = blocks[a, e]
+    def a2a(part, k):
+        return remote(
+            MSG.at[part, ex_to(k)], MSG_IN.at[part, ex], a2a_s.at[part, k], a2a_r.at[part, k], (dp, ex_to(k))
+        )
+
+    for part in range(PARTS):
+        for k in range(1, GROUPS):
+            a2a(part, k).start()
+    for part in range(PARTS):
+        MSG_IN[part, ex] = MSG[part, ex]
+
+    def arrive(a, part):
+        for k in range(1, GROUPS):
+            a2a(part, k).wait_recv()
+        flat = MSG_IN[part].reshape(SLOT_ROWS, D // 2)
+        for j in range(2):
+            rows = dot(place(SLOT_ROWS // PARTS, SLOT_ROWS, message_of_blocks, part, j), flat).astype(BF16)
+            rows = rows.reshape(2, LOCAL // PARTS, ROWS, D // 2)
+            for a in range(2):
+                for e in range(LOCAL // PARTS):
+                    R[a, 2 * part + e, c, y, x, :, j * (D // 2):(j + 1) * (D // 2)] = rows[a, e]
 
     def block_copy(a, e, py, px, sem, device):
         ref = R.at[a, e, c, py, px]
@@ -335,37 +340,45 @@
 
     for load in loads[3:]:
         load.wait()
+    def back(part, k):
+        return remote(
+            BACK.at[part, ex_to(k)], BACK_IN.at[part, ex], back_s.at[part, k], back_r.at[part, k], (dp, ex_to(k))
+        )
+
+    def send_back(a, part):
+        flat = halves(FIN[:, 2 * part:2 * part + 2].reshape(SLOT_ROWS // PARTS, D))
+        rows = [
+            dot(place(SLOT_ROWS // PARTS, SLOT_ROWS, message_of_blocks, part, j, True), flat[j]) for j in range(2)
+        ]
+        BACK[part] = (rows[0] + rows[1]).astype(BF16).reshape(GROUPS, ROWS, D // 2)
+        for k in range(1, GROUPS):
+            back(part, k).start()
+        BACK_IN[part, ex] = BACK[part, ex]
+
     steps = {
-        "G": lambda a, e: gather_first(a, e, start), "S": second, "O": second_on, "T": third, "X": expert,
-        "C": add_core, "D": add_second, "E": add_third, "F": add_fourth,
+        "A": arrive, "G": lambda a, e: gather_first(a, e, start), "S": second, "O": second_on, "T": third,
+        "X": expert, "C": add_core, "D": add_second, "E": add_third, "F": add_fourth, "B": send_back,
     }
     for line in ORDER:
         for word in line.split():
             steps[word[0]](int(word[1]), int(word[2]))
 
-    BACK[...] = (
-        dot(permutation(blocks_to_messages), FIN[...].reshape(2 * IMGS * SLOTS, D))
-        .astype(BF16).reshape(GROUPS, ROWS, D)
-    )
-
-    def back(k):
-        return remote(BACK.at[ex_to(k)], BACK_IN.at[ex], back_s.at[k], back_r.at[k], (dp, ex_to(k)))
-
-    for k in range(1, GROUPS):
-        back(k).start()
-    BACK_IN[ex] = BACK[ex]
-
     def grads(e, carry):
         weight_grads(e)
         return carry
 
     lax.fori_loop(0, LOCAL, grads, 0)
-    for k in range(1, GROUPS):
-        back(k).wait_recv()
-    SUMS[...] = (
-        dot(permutation(messages_to_slots), BACK_IN[...].reshape(2 * IMGS * SLOTS, D))
-        .astype(BF16).reshape(2, IMGS, SLOTS, D)
-    )
+    for part in range(PARTS):
+        for k in range(1, GROUPS):
+            back(part, k).wait_recv()
+    for j in range(2):
+        rows = [
+            dot(place(SLOT_ROWS, SLOT_ROWS, slots_of_message, part, j, True), BACK_IN[part].reshape(SLOT_ROWS, D // 2))
+            for part in range(PARTS)
+        ]
+        SUMS[:, :, :, j * (D // 2):(j + 1) * (D // 2)] = (
+            (rows[0] + rows[1]).astype(BF16).reshape(2, IMGS, SLOTS, D // 2)
+        )
 
     param = jnp.zeros((SLOTS, D), F32)
     logit_grads = []
@@ -379,8 +392,9 @@
         logit_grads.append(logit_grad)
         param = param + dot(logit_grad, T[i])
 
-    for j in range(GROUPS):
-        PP[j] = param[8 * (j // 2):8 * (j // 2) + 8, 640 * (j % 2):640 * (j % 2) + 640]
+    for j in range(GROUPS * SHARE):
+        tile = slice(8 * (j % SHARE), 8 * (j % SHARE) + 8)
+        PP[j // SHARE, tile] = param[8 * (j // 10):8 * (j // 10) + 8, 128 * (j % 10):128 * (j % 10) + 128]
 
     def ar_scatter(k):
         other, device = to_member(k)
@@ -404,14 +418,15 @@
     for k in range(1, GROUPS):
         ar_scatter(k).wait_recv()
         total = total + AR1[k - 1]
-    AR2[plane] = total
+    AR2[plane, :8 * SHARE] = total.astype(BF16)
+    AR2[plane, 8 * SHARE:] = jnp.zeros((8, 128), BF16)
     for k in range(1, NX * NY * NH):
         ar_plane(k).start()
     for k in range(1, NX * NY * NH):
         ar_plane(k).wait_recv()
-    total = AR2[0]
+    total = AR2[0, :8 * SHARE].astype(F32)
     for k in range(1, NX * NY * NH):
-        total = total + AR2[k]
+        total = total + AR2[k, :8 * SHARE].astype(F32)
     GP[member] = total
     for k in range(1, GROUPS):
         ar_gather(k).start()
@@ -437,8 +452,9 @@
 
     lax.fori_loop(0, LOCAL, drain, 0)
     for k in range(1, GROUPS):
-        a2a(k).wait_send()
-        back(k).wait_send()
+        for part in range(PARTS):
+            a2a(part, k).wait_send()
+            back(part, k).wait_send()
         ar_scatter(k).wait_send()
     for k in range(1, NX * NY * NH):
         ar_plane(k).wait_send()
@@ -446,8 +462,9 @@
         ar_gather(k).wait_recv()
     for k in range(1, GROUPS):
         ar_gather(k).wait_send()
-    for j in range(GROUPS):
-        grad_param[8 * (j // 2):8 * (j // 2) + 8, 640 * (j % 2):640 * (j % 2) + 640] = GP[j]
+    for j in range(GROUPS * SHARE):
+        tile = slice(8 * (j % SHARE), 8 * (j % SHARE) + 8)
+        grad_param[8 * (j // 10):8 * (j // 10) + 8, 128 * (j % 10):128 * (j % 10) + 128] = GP[j // SHARE, tile]
 
 
 def write_out(*refs):
@@ -460,7 +477,7 @@
 
 def on_device(tokens, slot_param, inner_weight, outer_weight, output_grad):
     vmem = pl.BlockSpec(memory_space=pltpu.VMEM)
-    chunk = (8, D * SLOTS // (8 * GROUPS))
+    chunk = (8 * SHARE, 128)
     dma = pltpu.SemaphoreType.DMA
     results = pl.pallas_call(
         kernel,
@@ -481,10 +498,10 @@
             pltpu.VMEM((IMGS, SLOTS, PATCHES), F32),
             pltpu.VMEM((IMGS, SLOTS, PATCHES), F32),
             pltpu.VMEM((2 * IMGS, SLOTS, D), BF16),
-            pltpu.VMEM((GROUPS, ROWS, D), BF16),
-            pltpu.VMEM((GROUPS, ROWS, D), BF16),
-            pltpu.VMEM((GROUPS, ROWS, D), BF16),
-            pltpu.VMEM((GROUPS, ROWS, D), BF16),
+            pltpu.VMEM((PARTS, GROUPS, ROWS, D // 2), BF16),
+            pltpu.VMEM((PARTS, GROUPS, ROWS, D // 2), BF16),
+            pltpu.VMEM((PARTS, GROUPS, ROWS, D // 2), BF16),
+            pltpu.VMEM((PARTS, GROUPS, ROWS, D // 2), BF16),
             pltpu.VMEM((2, LOCAL, ROWS, D), BF16),
             pltpu.VMEM((2, IMGS, SLOTS, D), BF16),
             pltpu.VMEM((2, LOCAL, NC, NY, NX, ROWS, D), BF16),
@@ -499,9 +516,9 @@
             pltpu.VMEM((LOCAL, NX - 1, NY, ROWS, D), BF16),
             pltpu.VMEM((GROUPS,) + chunk, F32),
             pltpu.VMEM((GROUPS - 1,) + chunk, F32),
-            pltpu.VMEM((NX * NY * NH,) + chunk, F32),
+            pltpu.VMEM((NX * NY * NH, 8 * SHARE + 8, 128), BF16),
             pltpu.VMEM((GROUPS,) + chunk, F32),
-            dma((5,)), dma((GROUPS,)), dma((GROUPS,)), dma((GROUPS,)), dma((GROUPS,)),
+            dma((5,)), dma((PARTS, GROUPS)), dma((PARTS, GROUPS)), dma((PARTS, GROUPS)), dma((PARTS, GROUPS)),
             dma((2, LOCAL, 8)), dma((2, LOCAL, 8)), dma((2, LOCAL, 6)), dma((2, LOCAL, 6)),
             dma((GROUPS,)), dma((GROUPS,)), dma((NX * NY * NH,)), dma((NX * NY * NH,)),
             dma((GROUPS,)), dma((GROUPS,)),

time: 87.8 us -> 84.4 us (0.961)
  Pallas kernels: 87 us -> 83.5 us
    pallas_call x1, Pallas kernels: 83.7 us -> 80.2 us  [on_device(): pl.pallas_call(kernel, out_shape=(pltpu.VMEM(tokens.shape, BF16), pltpu.V...]
where the time goes in v4:
time: 84.4 us; the launch traced here: 84.3 us
  Pallas kernels  83.5 us (99%)
    pallas_call x1, Pallas kernels, on_device(): pl.pallas_call(kernel, out_shape=(pltpu.VMEM(tokens.shape, BF16), pltpu.V...  80.2 us
    pallas_call x1, Pallas kernels, on_device(): pl.pallas_call(write_out, out_shape=tuple((jax.ShapeDtypeStruct(result.sh...  3.31 us

profile of v4, /device:TPU:1, one launch (start us, length us, event | category | flops | bytes accessed | tf_op | source)
XLA Modules:
  0.0 84.3 jit_solution(7680699779043170106)
XLA Ops:
  0.6 80.2 %shard_map.84 = (bf16[2,256,1280]{2,1,0:T(8,128)(2,1)S(1)}, f32[32,1280]{1,0:T(8,128)S(1)}, bf16[4,320,1280]{2,1,0:T(8,128)(2,1)S(1)}, bf16[4,320,1280]{2,1,0:T(8,128)(2,1)S(1)}) custom-call(bf16[2,256,1280]{2,1,0:T(8,128)(2,1)} %tokens.1, bf16[32,1280]{1,0:T(8,128)(2,1)} %slot_param.1, bf16[4,320,1280]{2,1,0:T(8,128)(2,1)} %inner.1, ...), custom_call_target="tpu_custom_call" | custom-call | tf_op jit(solution)/shard_map/pallas_call | solution.py:482
  80.8 3.3 %shard_map.85 = (bf16[2,256,1280]{2,1,0:T(8,128)(2,1)}, f32[32,1280]{1,0:T(8,128)}, bf16[4,320,1280]{2,1,0:T(8,128)(2,1)}, bf16[4,320,1280]{2,1,0:T(8,128)(2,1)}) custom-call(bf16[2,256,1280]{2,1,0:T(8,128)(2,1)S(1)} %get-tuple-element.8.refs_0_, f32[32,1280]{1,0:T(8,128)S(1)} %get-tuple-element.9.refs_1_, ...), custom_call_target="tpu_custom_call" | custom-call | tf_op jit(solution)/shard_map/pallas_call | solution.py:530

commit v5 on v4

--- a/solution.py
+++ b/solution.py
@@ -28,23 +28,23 @@
 SHARE = SLOTS * D // (8 * 128 * GROUPS)
 
 ORDER = (
-    "A00 G00 G11 G10",
-    "G01 A01 G02 G12",
-    "S00 S11 G13 S01",
-    "S10 G03 T00 S12",
-    "S02 O11 X00 O10",
-    "T01 C00 S13 O12",
-    "T11 X01 S03 T02",
-    "T10 X11 O13 C01",
-    "X02 T12 C11 X10",
-    "D00 X12 C10 T03",
-    "T13 C12 C02 D11",
-    "X03 X13 D01 C03",
-    "C13 D12 D10 E00",
-    "D13 D02 D03 E10",
-    "E11 E12 E13 E01",
-    "F10 F11 B00 E02",
-    "F12 E03 F13 B01",
+    "A00 G01 G00 G10",
+    "G11 A01 G12 G02",
+    "S01 S10 G13 S00",
+    "S11 G03 T01 O10",
+    "S02 S12 X01 O11",
+    "T00 S13 C01 T10",
+    "X00 O12 T11 S03",
+    "X10 T02 O13 C00",
+    "X11 C10 T12 X02",
+    "C11 D01 X12 C02",
+    "T03 D10 T13 C12",
+    "X03 D11 X13 C13",
+    "D00 C03 D12 D13",
+    "E11 D02 E10 E12",
+    "E01 D03 F10 E00",
+    "E13 F12 F11 B00",
+    "E02 F13 E03 B01",
 )
 
 
@@ -77,7 +77,7 @@
 def kernel(
     tokens, slot_param, inner, outer, cotangent,
     grad_tokens, grad_param, grad_inner, grad_outer,
-    T, G, SP, WI, WO, DI, CO, X, MSG, MSG_IN, BACK, BACK_IN, FIN, SUMS,
+    T, G, SP, WI, WO, DI, CO, X, MSG, MSG_IN, BACK, BACK_IN, FIN, SUMS, BY_BLOCK, BY_MESSAGE, BY_SLOT,
     R, ACT, SCA, SLOPE, PART, SIB, RY0, RX0, RY1, RX1,
     PP, AR1, AR2, GP,
     in_sem, a2a_s, a2a_r, back_s, back_r, ag_s, ag_r, rs_s, rs_r, ar_s, ar_r, mid_s, mid_r, last_s, last_r,
@@ -155,6 +155,11 @@
         CO[i] = combine
         X[i] = dot(dispatch.astype(BF16), T[i]).astype(BF16)
         X[IMGS + i] = dot(combine.astype(BF16), G[i]).astype(BF16)
+    for j in range(2):
+        BY_BLOCK[j] = place(SLOT_ROWS // PARTS, SLOT_ROWS, message_of_blocks, 0, j)
+        BY_MESSAGE[j] = place(SLOT_ROWS // PARTS, SLOT_ROWS, message_of_blocks, 0, j, True)
+        for part in range(PARTS):
+            BY_SLOT[part, j] = place(SLOT_ROWS, SLOT_ROWS, slots_of_message, part, j, True)
     flat = halves(X[...].reshape(SLOT_ROWS, D))
     for part in range(PARTS):
         rows = [dot(place(SLOT_ROWS, SLOT_ROWS, slots_of_message, part, j), flat[j]) for j in range(2)]
@@ -178,7 +183,7 @@
             a2a(part, k).wait_recv()
         flat = MSG_IN[part].reshape(SLOT_ROWS, D // 2)
         for j in range(2):
-            rows = dot(place(SLOT_ROWS // PARTS, SLOT_ROWS, message_of_blocks, part, j), flat).astype(BF16)
+            rows = dot(BY_BLOCK[j], flat).astype(BF16)
             rows = rows.reshape(2, LOCAL // PARTS, ROWS, D // 2)
             for a in range(2):
                 for e in range(LOCAL // PARTS):
@@ -347,9 +352,7 @@
 
     def send_back(a, part):
         flat = halves(FIN[:, 2 * part:2 * part + 2].reshape(SLOT_ROWS // PARTS, D))
-        rows = [
-            dot(place(SLOT_ROWS // PARTS, SLOT_ROWS, message_of_blocks, part, j, True), flat[j]) for j in range(2)
-        ]
+        rows = [dot(BY_MESSAGE[j], flat[j]) for j in range(2)]
         BACK[part] = (rows[0] + rows[1]).astype(BF16).reshape(GROUPS, ROWS, D // 2)
         for k in range(1, GROUPS):
             back(part, k).start()
@@ -368,17 +371,14 @@
         return carry
 
     lax.fori_loop(0, LOCAL, grads, 0)
-    for part in range(PARTS):
-        for k in range(1, GROUPS):
-            back(part, k).wait_recv()
+    for k in range(1, GROUPS):
+        back(0, k).wait_recv()
+    first = [dot(BY_SLOT[0, j], BACK_IN[0].reshape(SLOT_ROWS, D // 2)) for j in range(2)]
+    for k in range(1, GROUPS):
+        back(1, k).wait_recv()
     for j in range(2):
-        rows = [
-            dot(place(SLOT_ROWS, SLOT_ROWS, slots_of_message, part, j, True), BACK_IN[part].reshape(SLOT_ROWS, D // 2))
-            for part in range(PARTS)
-        ]
-        SUMS[:, :, :, j * (D // 2):(j + 1) * (D // 2)] = (
-            (rows[0] + rows[1]).astype(BF16).reshape(2, IMGS, SLOTS, D // 2)
-        )
+        rows = first[j] + dot(BY_SLOT[1, j], BACK_IN[1].reshape(SLOT_ROWS, D // 2))
+        SUMS[:, :, :, j * (D // 2):(j + 1) * (D // 2)] = rows.astype(BF16).reshape(2, IMGS, SLOTS, D // 2)
 
     param = jnp.zeros((SLOTS, D), F32)
     logit_grads = []
@@ -468,7 +468,10 @@
 
 
 def write_out(*refs):
-    copies = [pltpu.make_async_copy(refs[i], refs[4 + i], refs[8].at[i]) for i in range(4)]
+    pairs = [(refs[1], refs[5])]
+    for i in (0, 2, 3):
+        pairs += [(refs[i].at[j], refs[4 + i].at[j]) for j in range(refs[i].shape[0])]
+    copies = [pltpu.make_async_copy(*pair, refs[8].at[i]) for i, pair in enumerate(pairs)]
     for copy in copies:
         copy.start()
     for copy in copies:
@@ -504,6 +507,9 @@
             pltpu.VMEM((PARTS, GROUPS, ROWS, D // 2), BF16),
             pltpu.VMEM((2, LOCAL, ROWS, D), BF16),
             pltpu.VMEM((2, IMGS, SLOTS, D), BF16),
+            pltpu.VMEM((2, SLOT_ROWS // PARTS, SLOT_ROWS), BF16),
+            pltpu.VMEM((2, SLOT_ROWS, SLOT_ROWS // PARTS), BF16),
+            pltpu.VMEM((PARTS, 2, SLOT_ROWS, SLOT_ROWS), BF16),
             pltpu.VMEM((2, LOCAL, NC, NY, NX, ROWS, D), BF16),
             pltpu.VMEM((LOCAL, HIDDEN, BLOCKS * ROWS), BF16),
             pltpu.VMEM((LOCAL, HIDDEN, BLOCKS * ROWS), BF16),
@@ -532,7 +538,7 @@
         out_shape=tuple(jax.ShapeDtypeStruct(result.shape, result.dtype) for result in results),
         in_specs=[vmem] * 4,
         out_specs=(pl.BlockSpec(memory_space=pltpu.HBM),) * 4,
-        scratch_shapes=[dma((4,))],
+        scratch_shapes=[dma((1 + IMGS + 2 * LOCAL,))],
         compiler_params=pltpu.CompilerParams(vmem_limit_bytes=2**20),
     )(*[pltpu.with_memory_space_constraint(result, pltpu.VMEM) for result in results])
 

time: 84.4 us -> 83.8 us (level)
  no operation moved by 1% of the time
where the time goes in v5:
time: 83.8 us; the launch traced here: 83.7 us
  Pallas kernels  82.8 us (99%)
    pallas_call x1, Pallas kernels, on_device(): pl.pallas_call(kernel, out_shape=(pltpu.VMEM(tokens.shape, BF16), pltpu.V...  79.6 us
    pallas_call x1, Pallas kernels, on_device(): pl.pallas_call(write_out, out_shape=tuple((jax.ShapeDtypeStruct(result.sh...  3.29 us

profile of v5, /device:TPU:1, one launch (start us, length us, event | category | flops | bytes accessed | tf_op | source)
XLA Modules:
  0.0 83.7 jit_solution(3740696447606656072)
XLA Ops:
  0.6 79.6 %shard_map.84 = (bf16[2,256,1280]{2,1,0:T(8,128)(2,1)S(1)}, f32[32,1280]{1,0:T(8,128)S(1)}, bf16[4,320,1280]{2,1,0:T(8,128)(2,1)S(1)}, bf16[4,320,1280]{2,1,0:T(8,128)(2,1)S(1)}) custom-call(bf16[2,256,1280]{2,1,0:T(8,128)(2,1)} %tokens.1, bf16[32,1280]{1,0:T(8,128)(2,1)} %slot_param.1, bf16[4,320,1280]{2,1,0:T(8,128)(2,1)} %inner.1, ...), custom_call_target="tpu_custom_call" | custom-call | tf_op jit(solution)/shard_map/pallas_call | solution.py:485
  80.2 3.3 %shard_map.85 = (bf16[2,256,1280]{2,1,0:T(8,128)(2,1)}, f32[32,1280]{1,0:T(8,128)}, bf16[4,320,1280]{2,1,0:T(8,128)(2,1)}, bf16[4,320,1280]{2,1,0:T(8,128)(2,1)}) custom-call(bf16[2,256,1280]{2,1,0:T(8,128)(2,1)S(1)} %get-tuple-element.8.refs_0_, f32[32,1280]{1,0:T(8,128)S(1)} %get-tuple-element.9.refs_1_, ...), custom_call_target="tpu_custom_call" | custom-call | tf_op jit(solution)/shard_map/pallas_call | solution.py:536

commit v6 on v5

--- a/solution.py
+++ b/solution.py
@@ -13,6 +13,8 @@
 NX, NY, NC = 4, 2, 2
 NH, NZ = 2, 4
 GROUPS = NH * NZ
+FAR_FIRST = (6, 5, 7, 2, 4, 1, 3)
+PLANE_FAR_FIRST = (11, 9, 10, 7, 15, 8, 5, 13, 6, 14, 3, 1, 4, 12, 2)
 LOCAL = 4
 IMGS = 2
 SLOTS = GROUPS * LOCAL
@@ -102,10 +104,7 @@
     to_core = at_dp(x, y, 1 - c)
 
     def ex_to(k):
-        return (ex + k) % GROUPS
-
-    def ex_from(k):
-        return (ex + GROUPS - k) % GROUPS
+        return (h + k // NZ) % NH * NZ + (z + k) % NZ
 
     def remote(src, dst, send, recv, device):
         return pltpu.make_async_remote_copy(
@@ -116,12 +115,12 @@
     plane = (x * NY + y) * NH + h
 
     def to_member(k):
-        other = (member + k) % GROUPS
-        return other, ((x * NY + y) * NC + other // NZ, h * NZ + other % NZ)
+        core, depth = (c + k // NZ) % NC, (z + k) % NZ
+        return core * NZ + depth, ((x * NY + y) * NC + core, h * NZ + depth)
 
     def to_plane(k):
-        other = (plane + k) % (NX * NY * NH)
-        return (other // NH * NC + c, other % NH * NZ + z)
+        device = at_dp((x + k // 4) % NX, (y + k // 2) % NY, c)[0]
+        return device, (h + k) % NH * NZ + z
 
     barrier = pltpu.get_barrier_semaphore()
     partners = [
@@ -173,7 +172,7 @@
         )
 
     for part in range(PARTS):
-        for k in range(1, GROUPS):
+        for k in FAR_FIRST:
             a2a(part, k).start()
     for part in range(PARTS):
         MSG_IN[part, ex] = MSG[part, ex]
@@ -354,7 +353,7 @@
         flat = halves(FIN[:, 2 * part:2 * part + 2].reshape(SLOT_ROWS // PARTS, D))
         rows = [dot(BY_MESSAGE[j], flat[j]) for j in range(2)]
         BACK[part] = (rows[0] + rows[1]).astype(BF16).reshape(GROUPS, ROWS, D // 2)
-        for k in range(1, GROUPS):
+        for k in FAR_FIRST:
             back(part, k).start()
         BACK_IN[part, ex] = BACK[part, ex]
 
@@ -406,7 +405,7 @@
     def ar_gather(k):
         return remote(GP.at[member], GP.at[member], last_s.at[k], last_r.at[k], to_member(k)[1])
 
-    for k in range(1, GROUPS):
+    for k in FAR_FIRST:
         ar_scatter(k).start()
 
     for i in range(IMGS):
@@ -420,7 +419,7 @@
         total = total + AR1[k - 1]
     AR2[plane, :8 * SHARE] = total.astype(BF16)
     AR2[plane, 8 * SHARE:] = jnp.zeros((8, 128), BF16)
-    for k in range(1, NX * NY * NH):
+    for k in PLANE_FAR_FIRST:
         ar_plane(k).start()
     for k in range(1, NX * NY * NH):
         ar_plane(k).wait_recv()
@@ -428,7 +427,7 @@
     for k in range(1, NX * NY * NH):
         total = total + AR2[k, :8 * SHARE].astype(F32)
     GP[member] = total
-    for k in range(1, GROUPS):
+    for k in FAR_FIRST:
         ar_gather(k).start()
 
     def drain(e, carry):

time: 83.8 us -> 83.1 us (level)
  no operation moved by 1% of the time
where the time goes in v6:
time: 83.1 us; the launch traced here: 83 us
  Pallas kernels  82.2 us (99%)
    pallas_call x1, Pallas kernels, on_device(): pl.pallas_call(kernel, out_shape=(pltpu.VMEM(tokens.shape, BF16), pltpu.V...  78.9 us
    pallas_call x1, Pallas kernels, on_device(): pl.pallas_call(write_out, out_shape=tuple((jax.ShapeDtypeStruct(result.sh...  3.29 us

profile of v6, /device:TPU:1, one launch (start us, length us, event | category | flops | bytes accessed | tf_op | source)
XLA Modules:
  0.0 83.0 jit_solution(1162324439137916636)
XLA Ops:
  0.6 78.9 %shard_map.84 = (bf16[2,256,1280]{2,1,0:T(8,128)(2,1)S(1)}, f32[32,1280]{1,0:T(8,128)S(1)}, bf16[4,320,1280]{2,1,0:T(8,128)(2,1)S(1)}, bf16[4,320,1280]{2,1,0:T(8,128)(2,1)S(1)}) custom-call(bf16[2,256,1280]{2,1,0:T(8,128)(2,1)} %tokens.1, bf16[32,1280]{1,0:T(8,128)(2,1)} %slot_param.1, bf16[4,320,1280]{2,1,0:T(8,128)(2,1)} %inner.1, ...), custom_call_target="tpu_custom_call" | custom-call | tf_op jit(solution)/shard_map/pallas_call | solution.py:484
  79.6 3.3 %shard_map.85 = (bf16[2,256,1280]{2,1,0:T(8,128)(2,1)}, f32[32,1280]{1,0:T(8,128)}, bf16[4,320,1280]{2,1,0:T(8,128)(2,1)}, bf16[4,320,1280]{2,1,0:T(8,128)(2,1)}) custom-call(bf16[2,256,1280]{2,1,0:T(8,128)(2,1)S(1)} %get-tuple-element.8.refs_0_, f32[32,1280]{1,0:T(8,128)S(1)} %get-tuple-element.9.refs_1_, ...), custom_call_target="tpu_custom_call" | custom-call | tf_op jit(solution)/shard_map/pallas_call | solution.py:535

commit v7 on v6

--- a/solution.py
+++ b/solution.py
@@ -212,9 +212,9 @@
     def gather_on_left(e, act):
         act(block_copy(1, e, 1 - y, right(1), 5, to_x(3)))
 
-    def gather_third(a, e):
-        ref = R.at[a, e, c]
-        return remote(ref, ref, ag_s.at[a, e, 7], ag_r.at[a, e, 7], to_core)
+    def gather_third(a, e, j):
+        ref = R.at[a, e, c, (y + j) % NY]
+        return remote(ref, ref, ag_s.at[a, e, 7 + j], ag_r.at[a, e, 7 + j], to_core)
 
     def start(copy):
         copy.start()
@@ -230,6 +230,7 @@
             for k in (1, 3, 2):
                 wait_recv(0, e, k - 1)
                 gather_second_y(e, start, k)
+            gather_third(0, e, 0).start()
         else:
             wait_recv(1, e, 3)
             for k in (1, 3):
@@ -244,10 +245,13 @@
     def third(a, e):
         for sem in (3, 4, 5, 6) if a == 0 else (2, 1, 4, 5):
             wait_recv(a, e, sem)
-        gather_third(a, e).start()
+        if a == 1:
+            gather_third(1, e, 0).start()
+        gather_third(a, e, 1).start()
 
     def expert(a, e):
-        gather_third(a, e).wait_recv()
+        for j in range(NY):
+            gather_third(a, e, j).wait_recv()
         rows = R[a, e].reshape(BLOCKS * ROWS, D)
         if a == 0:
             hidden = dot(WI[e], rows, 1, 1)
@@ -433,7 +437,8 @@
     def drain(e, carry):
         for a in range(2):
             gather_first(a, e, wait_send)
-            gather_third(a, e).wait_send()
+            for j in range(NY):
+                gather_third(a, e, j).wait_send()
             sums_core(a, e).wait_send()
         gather_on_right(e, wait_send)
         gather_on_left(e, wait_send)
@@ -524,7 +529,7 @@
             pltpu.VMEM((NX * NY * NH, 8 * SHARE + 8, 128), BF16),
             pltpu.VMEM((GROUPS,) + chunk, F32),
             dma((5,)), dma((PARTS, GROUPS)), dma((PARTS, GROUPS)), dma((PARTS, GROUPS)), dma((PARTS, GROUPS)),
-            dma((2, LOCAL, 8)), dma((2, LOCAL, 8)), dma((2, LOCAL, 6)), dma((2, LOCAL, 6)),
+            dma((2, LOCAL, 9)), dma((2, LOCAL, 9)), dma((2, LOCAL, 6)), dma((2, LOCAL, 6)),
             dma((GROUPS,)), dma((GROUPS,)), dma((NX * NY * NH,)), dma((NX * NY * NH,)),
             dma((GROUPS,)), dma((GROUPS,)),
         ],

time: 83.1 us -> 82.8 us (level)
  no operation moved by 1% of the time
where the time goes in v7:
time: 82.8 us; the launch traced here: 82.6 us
  Pallas kernels  81.8 us (99%)
    pallas_call x1, Pallas kernels, on_device(): pl.pallas_call(kernel, out_shape=(pltpu.VMEM(tokens.shape, BF16), pltpu.V...  78.6 us
    pallas_call x1, Pallas kernels, on_device(): pl.pallas_call(write_out, out_shape=tuple((jax.ShapeDtypeStruct(result.sh...  3.29 us

profile of v7, /device:TPU:1, one launch (start us, length us, event | category | flops | bytes accessed | tf_op | source)
XLA Modules:
  0.0 82.6 jit_solution(7282572548768936525)
XLA Ops:
  0.6 78.6 %shard_map.84 = (bf16[2,256,1280]{2,1,0:T(8,128)(2,1)S(1)}, f32[32,1280]{1,0:T(8,128)S(1)}, bf16[4,320,1280]{2,1,0:T(8,128)(2,1)S(1)}, bf16[4,320,1280]{2,1,0:T(8,128)(2,1)S(1)}) custom-call(bf16[2,256,1280]{2,1,0:T(8,128)(2,1)} %tokens.1, bf16[32,1280]{1,0:T(8,128)(2,1)} %slot_param.1, bf16[4,320,1280]{2,1,0:T(8,128)(2,1)} %inner.1, ...), custom_call_target="tpu_custom_call" | custom-call | tf_op jit(solution)/shard_map/pallas_call | solution.py:489
  79.2 3.3 %shard_map.85 = (bf16[2,256,1280]{2,1,0:T(8,128)(2,1)}, f32[32,1280]{1,0:T(8,128)}, bf16[4,320,1280]{2,1,0:T(8,128)(2,1)}, bf16[4,320,1280]{2,1,0:T(8,128)(2,1)}) custom-call(bf16[2,256,1280]{2,1,0:T(8,128)(2,1)S(1)} %get-tuple-element.8.refs_0_, f32[32,1280]{1,0:T(8,128)S(1)} %get-tuple-element.9.refs_1_, ...), custom_call_target="tpu_custom_call" | custom-call | tf_op jit(solution)/shard_map/pallas_call | solution.py:540
